TPU v7x, 32 devices: a whole 2x2x4 slice. The times are simulated.
32 devices in a mesh: seq: 16 (over z, y, x), head: 2 (over core).
Axes of the slice: x: 2, y: 2, z: 4, core: 2. Of those that a mesh axis runs over, the one named last changes fastest.
Arguments:
- tokens: bfloat16 [32768, 512], P(('seq', 'head')), may hold values from -6 to 6
- first_values: bfloat16 [32768, 256], P(('seq', 'head')), may hold values from -6 to 6
- cotangent: bfloat16 [32768, 512], P(('seq', 'head')), may hold values from -6 to 6
- slot_count: int32 [16], P('seq'), may hold values from 1 to 8, as said below
- seq_lengths: int32 [16, 8], P('seq'), may hold values from 129 to 2048, as said below
- query_weight: bfloat16 [512, 512], replicated, may hold values from -0.5 to 0.5
- key_weight: bfloat16 [512, 512], replicated, may hold values from -0.25 to 0.25
- value_weight: bfloat16 [512, 256], replicated, may hold values from -0.25 to 0.25
- mixing_weight: bfloat16 [512, 512], replicated, may hold values from -1 to 1
- expand_weight: bfloat16 [512, 2048], replicated, may hold values from -0.25 to 0.25
- shrink_weight: bfloat16 [2048, 512], replicated, may hold values from -0.125 to 0.125
- expand_bias: float32 [2048], replicated, may hold values from -3 to 3
- before_gain: float32 [512], replicated, may hold values from 0.5 to 1.5
- before_shift: float32 [512], replicated, may hold values from -2 to 2
- middle_gain: float32 [512], replicated, may hold values from 0.5 to 1.5
- middle_shift: float32 [512], replicated, may hold values from -2 to 2
Outputs:
- output: bfloat16 [32768, 512], P(('seq', 'head'))
- input_grad: bfloat16 [32768, 512], P(('seq', 'head'))
- skip_grad: bfloat16 [32768, 256], P(('seq', 'head'))
- query_grad: float32 [512, 512], replicated
- key_grad: float32 [512, 512], replicated
- value_grad: float32 [512, 256], replicated
- mixing_grad: float32 [512, 512], replicated
- expand_grad: float32 [512, 2048], replicated
- shrink_grad: float32 [2048, 512], replicated
- bias_grad: float32 [2048], replicated
- before_gain_grad: float32 [512], replicated
- before_shift_grad: float32 [512], replicated
- middle_gain_grad: float32 [512], replicated
- middle_shift_grad: float32 [512], replicated
Inputs may be any that keep to these rules, and one draw needn't show every extreme that they name: `slot_count`: each bucket holds 1, 2, 4 or 8 sequences; the first bucket holds one and the second eight. `seq_lengths`: for a bucket of c sequences each slot below c holds a length above 2048 / (2 c) and at most 2048 / c; slots from c on are not read. The first bucket's sequence has 2048 tokens.
All inputs are finite; a program needn't handle non-finite values.
Results may differ from a plain program's by a relative error of at most 0.013.
The roundings to bfloat16 on the way count: a program that leaves them out, or rounds other values in their place, can miss the bound.
Values may be sent and summed in bfloat16 or wider, within the bound.
No kernel may reach another device: no remote copies, remote signals or barrier semaphores. Data moves between devices by JAX's collectives and lax.ppermute only.
A program may use at most 256 MiB of HBM per device.

v0:
```python
from functools import partial
import math

import jax
import jax.numpy as jnp
from jax import lax
from jax.sharding import PartitionSpec as P

HEADS = 8
HEAD_DIM = 64


epsilon = 1e-05
negative = -1e30


def shortened(array):
    return jax.tree.map(lambda a: a.astype(jnp.bfloat16) if a.dtype == jnp.float32 else a, array)


def layer_norm(row_values, norm_gain, norm_shift):
    average = jnp.mean(row_values, axis=-1, keepdims=True)
    centred = row_values - average
    spread = jnp.mean(centred * centred, axis=-1, keepdims=True)
    return centred * lax.rsqrt(spread + epsilon) * norm_gain + norm_shift


def gelu_tanh(values):
    return jax.nn.gelu(values, approximate=True)


def matmul(left_side, right_side):
    return jnp.dot(left_side, right_side, preferred_element_type=jnp.float32)


def left_matmul(left_side, right_side):
    return lax.dot_general(
        left_side, right_side, (((0,), (0,)), ((), ())), preferred_element_type=jnp.float32
    )


def right_matmul(left_side, right_side):
    return lax.dot_general(
        left_side, right_side, (((1,), (1,)), ((), ())), preferred_element_type=jnp.float32
    )


def slot_table(first_row, row_total, slot_count):
    indices = first_row + jnp.arange(row_total, dtype=jnp.int32)
    return (indices % slot_count[0], indices // slot_count[0])


def regroup(rows, slots, heads_here, head_width):
    seq_rows = rows.shape[0] // slots
    return rows.reshape(seq_rows, slots, heads_here, head_width).transpose(1, 0, 2, 3)


def ungroup(grouped):
    slots, seq_rows, columns = grouped.shape
    return grouped.transpose(1, 0, 2).reshape(seq_rows * slots, columns)


def causal_scores(query_group, key_group, offset, finish, scaling):
    query_block = query_group[:, offset:finish]
    key_block = key_group[:, :finish]
    scores = (
        jnp.einsum("cqhd,ckhd->chqk", query_block, key_block, preferred_element_type=jnp.float32)
        * scaling
    )
    query_index = offset + jnp.arange(finish - offset, dtype=jnp.int32)
    key_index = jnp.arange(finish, dtype=jnp.int32)
    allowed = key_index[None, :] <= query_index[:, None]
    return (jnp.where(allowed[None, None], scores, negative), query_block, key_block)


def forward_case(slots, heads_here, head_width, scaling, query_heads, key_heads, value_heads):
    seq_rows = query_heads.shape[0] // slots
    block = min(512, seq_rows)
    columns = heads_here * head_width
    query_group = regroup(query_heads, slots, heads_here, head_width)
    key_group = regroup(key_heads, slots, heads_here, head_width)
    value_group = regroup(value_heads, slots, heads_here, head_width)
    mixed_blocks = []
    logsum_blocks = []
    for offset in range(0, seq_rows, block):
        finish = offset + block
        scores, query_block, key_block = causal_scores(
            query_group, key_group, offset, finish, scaling
        )
        highest = jnp.max(scores, axis=-1, keepdims=True)
        raised = jnp.exp(scores - highest)
        row_total = jnp.sum(raised, axis=-1, keepdims=True)
        logsum_blocks.append((highest + jnp.log(row_total))[..., 0])
        weights = (raised / row_total).astype(jnp.bfloat16)
        mixed_part = jnp.einsum(
            "chqk,ckhd->cqhd", weights, value_group[:, :finish], preferred_element_type=jnp.float32
        )
        mixed_blocks.append(mixed_part.reshape(slots, block, columns).astype(jnp.bfloat16))
    mixed_heads = ungroup(jnp.concatenate(mixed_blocks, axis=1))
    logsum = jnp.concatenate(logsum_blocks, axis=2).reshape(-1)
    return (mixed_heads, logsum)


def backward_case(
    slots, heads_here, head_width, scaling, query_heads, key_heads, value_heads, grad_heads, logsum
):
    seq_rows = query_heads.shape[0] // slots
    block = min(512, seq_rows)
    columns = heads_here * head_width
    query_group = regroup(query_heads, slots, heads_here, head_width)
    key_group = regroup(key_heads, slots, heads_here, head_width)
    value_group = regroup(value_heads, slots, heads_here, head_width)
    grad_group = regroup(grad_heads, slots, heads_here, head_width)
    logsum_group = logsum.reshape(slots, heads_here, seq_rows)
    grad_query_blocks = []
    grad_key_total = jnp.zeros((slots, seq_rows, columns), jnp.float32)
    grad_value_total = jnp.zeros((slots, seq_rows, columns), jnp.float32)
    for offset in range(0, seq_rows, block):
        finish = offset + block
        scores, query_block, key_block = causal_scores(
            query_group, key_group, offset, finish, scaling
        )
        weights = jnp.exp(scores - logsum_group[:, :, offset:finish, None])
        grad_block = grad_group[:, offset:finish]
        grad_weights = jnp.einsum(
            "cqhd,ckhd->chqk",
            grad_block,
            value_group[:, :finish],
            preferred_element_type=jnp.float32,
        )
        inner_sum = jnp.sum(weights * grad_weights, axis=-1, keepdims=True)
        grad_scores = (weights * (grad_weights - inner_sum)).astype(jnp.bfloat16)
        grad_query_part = (
            jnp.einsum(
                "chqk,ckhd->cqhd", grad_scores, key_block, preferred_element_type=jnp.float32
            )
            * scaling
        )
        grad_query_blocks.append(grad_query_part.reshape(slots, block, columns))
        grad_key_part = (
            jnp.einsum(
                "chqk,cqhd->ckhd", grad_scores, query_block, preferred_element_type=jnp.float32
            )
            * scaling
        )
        grad_value_part = jnp.einsum(
            "chqk,cqhd->ckhd",
            weights.astype(jnp.bfloat16),
            grad_block,
            preferred_element_type=jnp.float32,
        )
        grad_key_total = grad_key_total.at[:, :finish].add(
            grad_key_part.reshape(slots, finish, columns)
        )
        grad_value_total = grad_value_total.at[:, :finish].add(
            grad_value_part.reshape(slots, finish, columns)
        )
    grad_query_heads = ungroup(jnp.concatenate(grad_query_blocks, axis=1)).astype(jnp.bfloat16)
    grad_key_heads = ungroup(grad_key_total).astype(jnp.bfloat16)
    grad_value_heads = ungroup(grad_value_total).astype(jnp.bfloat16)
    return (grad_query_heads, grad_key_heads, grad_value_heads)


def on_device(
    tokens,
    first_values,
    cotangent,
    slot_count,
    seq_lengths,
    query_weight,
    key_weight,
    value_weight,
    mixing_weight,
    expand_weight,
    shrink_weight,
    expand_bias,
    before_gain,
    before_shift,
    middle_gain,
    middle_shift,
):
    local_rows = tokens.shape[0]
    group_size = lax.axis_size("head")
    heads_here = HEADS // group_size
    head_width = HEAD_DIM
    scaling = 1.0 / math.sqrt(head_width)
    slot_local, position = slot_table(lax.axis_index("head") * local_rows, local_rows, slot_count)
    table = jnp.arange(seq_lengths.shape[1], dtype=jnp.int32)
    limit = jnp.sum(
        jnp.where(slot_local[:, None] == table[None, :], seq_lengths[0][None, :], 0), axis=1
    )
    valid_rows = (position < limit)[:, None]
    count_now = slot_count[0]
    case_index = (
        (count_now >= 2).astype(jnp.int32)
        + (count_now >= 4).astype(jnp.int32)
        + (count_now >= 8).astype(jnp.int32)
    )
    slot_options = (1, 2, 4, 8)
    inputs = tokens.astype(jnp.float32)
    normed, before_back = jax.vjp(layer_norm, inputs, before_gain, before_shift)
    normed_low = normed.astype(jnp.bfloat16)
    query_local = matmul(normed_low, query_weight).astype(jnp.bfloat16)
    key_local = matmul(normed_low, key_weight).astype(jnp.bfloat16)
    fresh_local = matmul(normed_low, value_weight).astype(jnp.bfloat16)
    query_heads, key_heads, fresh_heads, skip_heads = (
        lax.all_to_all(query_local, "head", split_axis=1, concat_axis=0, tiled=True),
        lax.all_to_all(key_local, "head", split_axis=1, concat_axis=0, tiled=True),
        lax.all_to_all(fresh_local, "head", split_axis=1, concat_axis=0, tiled=True),
        lax.all_to_all(first_values, "head", split_axis=1, concat_axis=0, tiled=True),
    )
    value_heads = jnp.concatenate([fresh_heads, skip_heads], axis=1)
    forward_cases = [
        partial(forward_case, option, heads_here, head_width, scaling) for option in slot_options
    ]
    mixed_heads, logsum = lax.switch(case_index, forward_cases, query_heads, key_heads, value_heads)
    mixed_local = jax.tree.map(
        lambda part, own: part.astype(own.dtype),
        lax.all_to_all(shortened(mixed_heads), "head", split_axis=0, concat_axis=1, tiled=True),
        mixed_heads,
    )
    after = inputs + matmul(mixed_local, mixing_weight)
    middle, middle_back = jax.vjp(layer_norm, after, middle_gain, middle_shift)
    middle_low = middle.astype(jnp.bfloat16)
    pre_act = matmul(middle_low, expand_weight) + expand_bias
    active, gelu_back = jax.vjp(gelu_tanh, pre_act)
    active_low = active.astype(jnp.bfloat16)
    grown = matmul(active_low, shrink_weight)
    output = jnp.where(valid_rows, after + grown, 0.0).astype(jnp.bfloat16)
    grad_out = jnp.where(valid_rows, cotangent.astype(jnp.float32), 0.0)
    grad_out_low = grad_out.astype(jnp.bfloat16)
    shrink_grad = left_matmul(active_low, grad_out_low)
    grad_active = right_matmul(grad_out_low, shrink_weight)
    (grad_pre,) = gelu_back(grad_active)
    grad_pre_low = grad_pre.astype(jnp.bfloat16)
    ones_rows = jnp.ones((local_rows,), jnp.bfloat16)
    bias_grad = jnp.dot(ones_rows, grad_pre_low, preferred_element_type=jnp.float32)
    expand_grad = left_matmul(middle_low, grad_pre_low)
    grad_middle = right_matmul(grad_pre_low, expand_weight)
    grad_after_part, middle_gain_grad, middle_shift_grad = middle_back(grad_middle)
    grad_after = grad_out + grad_after_part
    grad_after_low = grad_after.astype(jnp.bfloat16)
    mixing_grad = left_matmul(mixed_local, grad_after_low)
    grad_mixed = right_matmul(grad_after_low, mixing_weight).astype(jnp.bfloat16)
    grad_heads = lax.all_to_all(grad_mixed, "head", split_axis=1, concat_axis=0, tiled=True)
    backward_cases = [
        partial(backward_case, option, heads_here, head_width, scaling) for option in slot_options
    ]
    grad_query_heads, grad_key_heads, grad_value_heads = lax.switch(
        case_index, backward_cases, query_heads, key_heads, value_heads, grad_heads, logsum
    )
    half_columns = heads_here * head_width // 2
    grad_fresh_heads = grad_value_heads[:, :half_columns]
    grad_skip_heads = grad_value_heads[:, half_columns:]
    back_query, back_key, back_fresh, skip_grad = (
        lax.all_to_all(
            shortened(grad_query_heads), "head", split_axis=0, concat_axis=1, tiled=True
        ).astype(grad_query_heads.dtype),
        lax.all_to_all(
            shortened(grad_key_heads), "head", split_axis=0, concat_axis=1, tiled=True
        ).astype(grad_key_heads.dtype),
        lax.all_to_all(
            shortened(grad_fresh_heads), "head", split_axis=0, concat_axis=1, tiled=True
        ).astype(grad_fresh_heads.dtype),
        lax.all_to_all(
            shortened(grad_skip_heads), "head", split_axis=0, concat_axis=1, tiled=True
        ).astype(grad_skip_heads.dtype),
    )
    query_grad = left_matmul(normed_low, back_query)
    key_grad = left_matmul(normed_low, back_key)
    value_grad = left_matmul(normed_low, back_fresh)
    grad_normed = (
        right_matmul(back_query, query_weight)
        + right_matmul(back_key, key_weight)
        + right_matmul(back_fresh, value_weight)
    )
    grad_input_part, before_gain_grad, before_shift_grad = before_back(grad_normed)
    input_grad = (grad_after + grad_input_part).astype(jnp.bfloat16)
    gradients = (
        query_grad,
        key_grad,
        value_grad,
        mixing_grad,
        expand_grad,
        shrink_grad,
        bias_grad,
        before_gain_grad,
        before_shift_grad,
        middle_gain_grad,
        middle_shift_grad,
    )
    summed = lax.psum(
        (
            gradients[0],
            gradients[1],
            gradients[2],
            gradients[3],
            gradients[4],
            gradients[5],
            gradients[6],
            gradients[7],
            gradients[8],
            gradients[9],
            gradients[10],
        ),
        ("seq", "head"),
    )
    return (
        output,
        input_grad,
        skip_grad,
        summed[0],
        summed[1],
        summed[2],
        summed[3],
        summed[4],
        summed[5],
        summed[6],
        summed[7],
        summed[8],
        summed[9],
        summed[10],
    )


def solution(mesh):
    placed = (
        P(("seq", "head"), None),
        P(("seq", "head"), None),
        P(("seq", "head"), None),
        P("seq"),
        P("seq", None),
        P(),
        P(),
        P(),
        P(),
        P(),
        P(),
        P(),
        P(),
        P(),
        P(),
        P(),
    )
    return jax.shard_map(
        on_device,
        mesh=mesh,
        in_specs=placed,
        out_specs=(
            P(("seq", "head"), None),
            P(("seq", "head"), None),
            P(("seq", "head"), None),
            P(),
            P(),
            P(),
            P(),
            P(),
            P(),
            P(),
            P(),
            P(),
            P(),
            P(),
        ),
        check_vma=False,
    )
```

profile of v0, /device:TPU:0, one launch (start us, length us, event | category | flops | bytes accessed | tf_op | source)
XLA Modules:
  0.0 620.9 jit_solution(15590827902238466179)
XLA Ops:
  14.3 4.2 all-to-all-start.2
  24.2 4.4 all-to-all-start.1
  33.7 4.4 all-to-all-start
  40.4 4.2 all-to-all-start.3
  49.2 70.6 %conditional.2 = (f32[8192]{0:T(1024)S(1)}, bf16[2048,256]{1,0:T(8,128)(2,1)}) conditional(s32[]{:T(128)} %clamp.4, (bf16[2048,256]{1,0:T(8,128)(2,1)}, bf16[2048,256]{1,0:T(8,128)(2,1)S(1)}, bf16[2048,256]{1,0:T(8,128)(2,1)}) %tuple.234, (bf16[2048,256]{1,0:T(8,128)(2,1)}, bf16[2048,256]{1,0:T(8,128)(2,1)S(1)}, ...), branch_computations={%region_3.12_spmd, %region_12.17_spmd, %region_17.20_spmd, %region... | conditional | flops 2817541632 | bytes 180760784 | solution.py:216
  73.7 4.0 fusion.3
  77.7 4.0 fusion.14
  84.9 4.3 fusion.1
  89.3 4.7 fusion.15
  119.8 4.6 all-to-all-start.4
  133.5 4.4 fusion.189
  137.9 7.7 %fusion.156 = bf16[1024,2048]{1,0:T(8,128)(2,1)S(1)} fusion(f32[1024,2048]{1,0:T(8,128)S(1)} %fusion.189, f32[2048]{0:T(1024)S(1)} %copy-done.92, bf16[2048,512]{1,0:T(8,128)(2,1)S(1)} %copy-done.91, bf16[1024,512]{0,1:T(8,128)(2,1)S(1)} %copy-done.35, pred[1024]{0:T(1024)(128)(4,1)S(1)} %fusion.174), kind=kOutput, calls=%fused_computation.286 | convolution fusion | flops 2193096704 | bytes 15737856 | tf_op jit(solution)/shard_map/dot_general | solution.py:43
  145.6 4.3 fusion.195
  161.1 5.4 all_to_all.190
  168.7 137.6 %conditional.3 = (bf16[2048,256]{1,0:T(8,128)(2,1)S(1)}, bf16[2048,256]{1,0:T(8,128)(2,1)}, bf16[2048,256]{1,0:T(8,128)(2,1)}) conditional(s32[]{:T(128)} %clamp.4, (bf16[2048,256]{1,0:T(8,128)(2,1)S(1)}, bf16[2048,256]{1,0:T(8,128)(2,1)S(1)}, f32[8192]{0:T(1024)S(1)}, bf16[2048,256]{1,0:T(8,128)(2,1)}, ...), branch_computations={%region_27.32_spmd, %region_32.35_spmd, %region_35.37_spmd, %regio... | conditional | flops 6861874688 | bytes 505704832 | solution.py:249
  195.3 3.7 multiply_convert_fusion.2
  205.2 7.3 %multiply_reduce_fusion.1 = (f32[4,512]{1,0:T(4,128)S(1)}, f32[4,512,1536]{2,1,0:T(8,128)}) fusion(f32[4,512,1536]{2,1,0:T(8,128)S(1)} %fusion.92, f32[4,512]{1,0:T(4,128)S(1)} %get-tuple-element.559, bf16[1,2048,4,64]{1,3,2,0:T(8,128)(2,1)S(1)} %bitcast.546, bf16[1,2048,4,64]{1,3,2,0:T(8,128)(2,1)S(1)} %bitcast.560, pred[512,1536]{1,0:T(8,128)(4,1)S(1)} %copy-done.57), kind=kOutput, calls=%fused_computation.130 | convolution fusion | flops 418379776 | bytes 27017216 | tf_op jit(solution)/shard_map/cond/branch_0_fun/cqhd,ckhd->chqk/dot_general | solution.py:67
  212.5 5.7 multiply_convert_fusion.1
  218.2 5.9 fusion.76
  231.2 8.4 %fusion.73 = f32[4,2048,64]{1,2,0:T(8,128)} fusion(f32[4,512,2048]{2,1,0:T(8,128)S(1)} %fusion.97, f32[4,512]{1,0:T(4,128)S(1)} %get-tuple-element.558, pred[512,2048]{1,0:T(8,128)(4,1)} %iota_compare_fusion.8, bf16[1,2048,4,64]{1,3,2,0:T(8,128)(2,1)} %bitcast.584), kind=kOutput, calls=%fused_computation.136 | convolution fusion | flops 553648128 | bytes 20193280 | tf_op jit(solution)/shard_map/cond/branch_0_fun/chqk,cqhd->ckhd/dot_general | solution.py:146
  244.7 12.7 %multiply_reduce_fusion = (f32[4,512]{1,0:T(4,128)S(1)}, f32[4,512,2048]{2,1,0:T(8,128)}) fusion(f32[4,512,2048]{2,1,0:T(8,128)} %copy-done.3, f32[4,512]{1,0:T(4,128)S(1)} %get-tuple-element.558, pred[512,2048]{1,0:T(8,128)(4,1)} %iota_compare_fusion.8, bf16[2048,4,64]{0,2,1:T(8,128)(2,1)S(1)} %bitcast.541, bf16[1,2048,4,64]{1,3,2,0:T(8,128)(2,1)} %bitcast.585), kind=kOutput, calls=%fused_computation.127 | convolution fusion | flops 557840384 | bytes 35930112 | tf_op jit(solution)/shard_map/cond/branch_0_fun/cqhd,ckhd->chqk/dot_general | solution.py:125
  257.4 12.2 %multiply_convert_fusion = bf16[4,512,2048]{2,1,0:T(8,128)(2,1)S(1)} fusion(f32[4,512,2048]{2,1,0:T(8,128)} %get-tuple-element.562, f32[4,512,2048]{2,1,0:T(8,128)} %copy-done.3, f32[4,512]{1,0:T(4,128)S(1)} %get-tuple-element.561, f32[4,512]{1,0:T(4,128)S(1)} %get-tuple-element.558, pred[512,2048]{1,0:T(8,128)(4,1)S(1)} %copy-done.31), kind=kLoop, calls=%fused_computation.126 | loop fusion | flops 25165824 | bytes 43008000 | tf_op jit(solution)/shard_map/cond/branch_0_fun/convert_element_type | solution.py:132
  307.3 4.4 all-to-all-start.7
  311.8 10.0 %fusion.170 = f32[2048,512]{1,0:T(8,128)} fusion(bf16[1024,512]{0,1:T(8,128)(2,1)} %copy.359, pred[1024]{0:T(1024)(128)(4,1)S(1)} %copy-done.85, f32[1024,2048]{1,0:T(8,128)} %copy-done.96, f32[2048]{0:T(1024)S(1)} %copy-done.93), kind=kOutput, calls=%fused_computation.320 | convolution fusion | flops 2170028032 | bytes 13640704 | tf_op jit(solution)/shard_map/dot_general | solution.py:37
  321.9 4.5 fusion.188
  328.1 4.4 all-to-all-start.6
  337.1 4.2 all-to-all-start.8
  353.9 4.4 all-to-all-start.9
  358.3 8.8 %select_convert_fusion = bf16[1024,512]{0,1:T(8,128)(2,1)} fusion(f32[1024,512]{0,1:T(8,128)S(1)} %copy-done.14, bf16[2048,512]{1,0:T(8,128)(2,1)} %param.82, pred[1024]{0:T(1024)(128)(4,1)S(1)} %copy-done.85, f32[1024,2048]{1,0:T(8,128)} %copy-done.96, f32[2048]{0:T(1024)S(1)} %copy-done.93), kind=kOutput, calls=%fused_computation.311 | convolution fusion | flops 2170028032 | bytes 13640704 | tf_op jit(solution)/shard_map/dot_general | solution.py:33
  381.2 53.0 %all-reduce.4 = (f32[2048]{0:T(1024)}, f32[512]{0:T(512)}, f32[512]{0:T(512)}, f32[512]{0:T(512)}, f32[512]{0:T(512)}) all-reduce(f32[2048]{0:T(1024)S(1)} %bitcast.671, f32[512]{0:T(512)S(1)} %get-tuple-element.518, f32[512]{0:T(512)S(1)} %get-tuple-element.520, ...), channel_id=1, replica_groups=mesh['seq'=16,'head'=2] {'seq','head'}, use_global_device_ids=true, to_apply=%region_47.48 | all-reduce | flops 4096 | bytes 32768 | tf_op jit(solution)/shard_map/psum | solution.py:292
  436.1 162.0 %all-reduce.8.cloned.1.call-done = (f32[512,512]{1,0:T(8,128)}, f32[512,512]{1,0:T(8,128)}, f32[512,256]{1,0:T(8,128)}, f32[512,512]{1,0:T(8,128)}, f32[512,2048]{1,0:T(8,128)}, /*index=5*/f32[2048,512]{1,0:T(8,128)}) async-done(((f32[512,512]{1,0:T(8,128)}, f32[512,512]{1,0:T(8,128)}, f32[512,256]{1,0:T(8,128)}, f32[512,512]{1,0:T(8,128)}, f32[512,2048]{1,0:T(8,128)}, /*index=5*/f32[2048,512]{1,0:T(8,128)}), ...) | async-done | bytes 12058640 | tf_op jit(solution)/shard_map/psum | solution.py:292
  607.1 4.7 copy.488
  (276 shorter events, 177.4 us)
Async XLA Ops:
  7.2 126.3 %copy-start = (bf16[512,2048]{1,0:T(8,128)(2,1)S(1)}, bf16[512,2048]{1,0:T(8,128)(2,1)}, u32[]{:S(2)}) copy-start(bf16[512,2048]{1,0:T(8,128)(2,1)} %param.81) | copy-start | bytes 6291460
  8.8 24.9 %copy-start.10 = (bf16[1024,512]{0,1:T(8,128)(2,1)}, bf16[1024,512]{0,1:T(8,128)(2,1)S(1)}, u32[]{:S(2)}) copy-start(bf16[1024,512]{0,1:T(8,128)(2,1)S(1)} %copy.348) | copy-start | bytes 3145732
  14.3 9.9 %all-to-all-start.2 = ((bf16[1024,2,128]{0,2,1:T(8,128)(2,1)}), bf16[1024,2,128]{0,2,1:T(8,128)(2,1)}, u32[]{:S(2)}, u32[]{:S(2)}) async-start(bf16[1024,2,128]{0,2,1:T(8,128)(2,1)} %bitcast.618), calls=%async_computation.2 | async-start | bytes 1048576 | tf_op jit(solution)/shard_map/all_to_all | solution.py:209
  24.2 9.6 %all-to-all-start.1 = ((bf16[1024,2,256]{0,2,1:T(8,128)(2,1)}), bf16[1024,2,256]{0,2,1:T(8,128)(2,1)}, u32[]{:S(2)}, u32[]{:S(2)}) async-start(bf16[1024,2,256]{0,2,1:T(8,128)(2,1)} %bitcast.642), calls=%async_computation.1 | async-start | bytes 2097152 | tf_op jit(solution)/shard_map/all_to_all | solution.py:208
  33.7 6.7 %all-to-all-start = ((bf16[1024,2,256]{0,2,1:T(8,128)(2,1)}), bf16[1024,2,256]{0,2,1:T(8,128)(2,1)}, u32[]{:S(2)}, u32[]{:S(2)}) async-start(bf16[1024,2,256]{0,2,1:T(8,128)(2,1)} %bitcast.643), calls=%async_computation | async-start | bytes 2097152 | tf_op jit(solution)/shard_map/all_to_all | solution.py:207
  40.4 6.5 %all-to-all-start.3 = ((bf16[1024,2,128]{2,0,1:T(8,128)(2,1)}), bf16[1024,2,128]{2,0,1:T(8,128)(2,1)}, u32[]{:S(2)}, u32[]{:S(2)}) async-start(bf16[1024,2,128]{2,0,1:T(8,128)(2,1)} %copy_bitcast_fusion.1), calls=%async_computation.3 | async-start | bytes 1048576 | tf_op jit(solution)/shard_map/all_to_all | solution.py:210
  119.8 13.5 %copy-start.90 = (s32[1,8]{1,0:T(1,128)S(1)}, s32[1,8]{1,0:T(1,128)}, u32[]{:S(2)}) copy-start(s32[1,8]{1,0:T(1,128)} %param.76) | copy-start | bytes 100
  119.8 13.7 %copy-start.86 = (f32[512]{0:T(512)S(1)}, f32[512]{0:T(512)}, u32[]{:S(2)}) copy-start(f32[512]{0:T(512)} %param.86) | copy-start | bytes 6148
  119.8 13.7 %copy-start.94 = (f32[512]{0:T(512)S(1)}, f32[512]{0:T(512)}, u32[]{:S(2)}) copy-start(f32[512]{0:T(512)} %param.87) | copy-start | bytes 6148
  119.8 6.9 %all-to-all-start.4 = ((bf16[2,1024,256]{2,1,0:T(8,128)(2,1)}), bf16[2,1024,256]{2,1,0:T(8,128)(2,1)}, u32[]{:S(2)}, u32[]{:S(2)}) async-start(bf16[2,1024,256]{2,1,0:T(8,128)(2,1)} %bitcast.606), calls=%async_computation.4 | async-start | bytes 2097152 | tf_op jit(solution)/shard_map/all_to_all | solution.py:219
  131.4 24.1 %copy-start.75 = (f32[1024]{0:T(1024)}, f32[1024]{0:T(1024)S(1)}, u32[]{:S(2)}) copy-start(f32[1024]{0:T(1024)S(1)} %broadcast_multiply_fusion) | copy-start | bytes 12292
  133.0 22.5 %copy-start.81 = (f32[1024]{0:T(1024)}, f32[1024]{0:T(1024)S(1)}, u32[]{:S(2)}) copy-start(f32[1024]{0:T(1024)S(1)} %fusion.182) | copy-start | bytes 12292
  133.5 25.1 %copy-start.84 = (pred[1024]{0:T(1024)(128)(4,1)}, pred[1024]{0:T(1024)(128)(4,1)S(1)}, u32[]{:S(2)}) copy-start(pred[1024]{0:T(1024)(128)(4,1)S(1)} %fusion.174) | copy-start | bytes 3076
  155.5 13.1 %copy-start.4 = (bf16[2,1024,256]{2,1,0:T(8,128)(2,1)S(1)}, bf16[2,1024,256]{2,1,0:T(8,128)(2,1)}, u32[]{:S(2)}) copy-start(bf16[2,1024,256]{2,1,0:T(8,128)(2,1)} %copy.349) | copy-start | bytes 3145732
  155.6 13.1 %copy-start.5 = (bf16[2048,256]{1,0:T(8,128)(2,1)S(1)}, bf16[2048,256]{1,0:T(8,128)(2,1)}, u32[]{:S(2)}) copy-start(bf16[2048,256]{1,0:T(8,128)(2,1)} %pad_maximum_fusion) | copy-start | bytes 3145732
  158.5 10.2 %copy-start.79 = (f32[1024]{0:T(1024)}, f32[1024]{0:T(1024)S(1)}, u32[]{:S(2)}) copy-start(f32[1024]{0:T(1024)S(1)} %negate_multiply_fusion.1) | copy-start | bytes 12292
  168.7 143.0 %copy-start.85 = (pred[1024]{0:T(1024)(128)(4,1)S(1)}, pred[1024]{0:T(1024)(128)(4,1)}, u32[]{:S(2)}) copy-start(pred[1024]{0:T(1024)(128)(4,1)} %copy-done.84) | copy-start | bytes 3076
  168.7 143.0 %copy-start.93 = (f32[2048]{0:T(1024)S(1)}, f32[2048]{0:T(1024)}, u32[]{:S(2)}) copy-start(f32[2048]{0:T(1024)} %param.83) | copy-start | bytes 24580
  244.7 12.7 %copy-start.31 = (pred[512,2048]{1,0:T(8,128)(4,1)S(1)}, pred[512,2048]{1,0:T(8,128)(4,1)}, u32[]{:S(2)}) copy-start(pred[512,2048]{1,0:T(8,128)(4,1)} %iota_compare_fusion.8) | copy-start | bytes 3145732 | tf_op jit(solution)/shard_map/cond
  257.4 12.2 %copy-start.26 = (bf16[2048,256]{0,1:T(8,128)(2,1)S(1)}, bf16[2048,256]{0,1:T(8,128)(2,1)}, u32[]{:S(2)}) copy-start(bf16[2048,256]{0,1:T(8,128)(2,1)} %copy-done.23) | copy-start | bytes 3145732 | tf_op jit(solution)/shard_map/cond
  307.3 20.9 %all-to-all-start.7 = ((bf16[2,1024,256]{2,1,0:T(8,128)(2,1)}), bf16[2,1024,256]{2,1,0:T(8,128)(2,1)}, u32[]{:S(2)}, u32[]{:S(2)}) async-start(bf16[2,1024,256]{2,1,0:T(8,128)(2,1)} %bitcast.202), calls=%async_computation.7 | async-start | bytes 2097152 | tf_op jit(solution)/shard_map/all_to_all | solution.py:259
  311.7 10.1 %copy-start.14 = (f32[1024,512]{0,1:T(8,128)S(1)}, f32[1024,512]{0,1:T(8,128)}, u32[]{:S(2)}) copy-start(f32[1024,512]{0,1:T(8,128)} %copy-done.13) | copy-start | bytes 6291460
  311.7 10.1 %copy-start.52 = (bf16[1024,2048]{1,0:T(8,128)(2,1)S(1)}, bf16[1024,2048]{1,0:T(8,128)(2,1)}, u32[]{:S(2)}) copy-start(bf16[1024,2048]{1,0:T(8,128)(2,1)} %copy-done.51) | copy-start | bytes 12582916
  311.7 10.1 %copy-start.76 = (f32[1024]{0:T(1024)S(1)}, f32[1024]{0:T(1024)}, u32[]{:S(2)}) copy-start(f32[1024]{0:T(1024)} %copy-done.75) | copy-start | bytes 12292
  311.8 10.1 %copy-start.82 = (f32[1024]{0:T(1024)S(1)}, f32[1024]{0:T(1024)}, u32[]{:S(2)}) copy-start(f32[1024]{0:T(1024)} %copy-done.81) | copy-start | bytes 12292
  326.4 17.2 %copy-start.33 = (bf16[1024,512]{0,1:T(8,128)(2,1)S(1)}, bf16[1024,512]{0,1:T(8,128)(2,1)}, u32[]{:S(2)}) copy-start(bf16[1024,512]{0,1:T(8,128)(2,1)} %copy-done.32) | copy-start | bytes 3145732
  328.1 8.9 %all-to-all-start.6 = ((bf16[2,1024,256]{2,1,0:T(8,128)(2,1)}), bf16[2,1024,256]{2,1,0:T(8,128)(2,1)}, u32[]{:S(2)}, u32[]{:S(2)}) async-start(bf16[2,1024,256]{2,1,0:T(8,128)(2,1)} %bitcast.604), calls=%async_computation.6 | async-start | bytes 2097152 | tf_op jit(solution)/shard_map/all_to_all | solution.py:256
  337.1 12.4 %all-to-all-start.8 = ((bf16[2,1024,128]{2,1,0:T(8,128)(2,1)}), bf16[2,1024,128]{2,1,0:T(8,128)(2,1)}, u32[]{:S(2)}, u32[]{:S(2)}) async-start(bf16[2,1024,128]{2,1,0:T(8,128)(2,1)} %bitcast.630), calls=%async_computation.8 | async-start | bytes 1048576 | tf_op jit(solution)/shard_map/all_to_all | solution.py:262
  341.3 256.8 %all-reduce.8.cloned.1.call-start = ((), (), s32[]{:S(2)}) async-start(), calls=%async_computation.10 | async-start | bytes 24117248 | tf_op jit(solution)/shard_map/psum | solution.py:292
  353.9 80.3 %all-to-all-start.9 = ((bf16[2,1024,128]{2,1,0:T(8,128)(2,1)}), bf16[2,1024,128]{2,1,0:T(8,128)(2,1)}, u32[]{:S(2)}, u32[]{:S(2)}) async-start(bf16[2,1024,128]{2,1,0:T(8,128)(2,1)} %bitcast.208), calls=%async_computation.9 | async-start | bytes 1048576 | tf_op jit(solution)/shard_map/all_to_all | solution.py:265
  358.3 11.3 %copy-start.69 = (bf16[512,512]{1,0:T(8,128)(2,1)S(1)}, bf16[512,512]{1,0:T(8,128)(2,1)}, u32[]{:S(2)}) copy-start(bf16[512,512]{1,0:T(8,128)(2,1)} %param.77) | copy-start | bytes 1572868
  598.1 13.7 %copy-start.53 = (f32[2048,512]{1,0:T(8,128)S(1)}, f32[2048,512]{1,0:T(8,128)}, u32[]{:S(2)}) copy-start(f32[2048,512]{1,0:T(8,128)} %get-tuple-element.616) | copy-start | bytes 12582916
  (50 other events, 244.0 us)
Sparse Core Ops, SparseCore 0:
  354.0 244.0 all-reduce.7
where the time goes:
time: 628 us; the launch traced here: 621 us
  waiting for transfers between devices  163 us (26%)
  matrix products  157 us (25%)
  local copies, waits for them, and re-layouts  72.9 us (12%)
  other arithmetic  63.7 us (10%)
  blocking collectives  58.4 us (9%)
  loops' own time  50.6 us (8%)
  starting transfers between devices  39.4 us (6%)
  between operations  15.8 us (3%)
    psum x1, waiting for transfers between devices, on_device(): lax.psum((gradients[0], gradients[1], gradients[2], gradients[3], gradien...  162 us
    psum x1, blocking collectives, on_device(): lax.psum((gradients[0], gradients[1], gradients[2], gradients[3], gradien...  53 us
    unnamed x116, local copies, waits for them, and re-layouts  28.7 us
    another operation x1, loops' own time, on_device(): lax.switch(case_index, backward_cases, query_heads, key_heads, value_head...  27.9 us
    dot_general x6, matrix products, left_matmul(): lax.dot_general(left_side, right_side, (((0,), (0,)), ((), ())), preferre...  24.5 us
    dot_general x6, matrix products, matmul(): return jnp.dot(left_side, right_side, preferred_element_type=jnp.float32)  24.1 us
    convert_element_type x4, other arithmetic, backward_case(): grad_scores = (weights * (grad_weights - inner_sum)).astype(jnp.bfloat16)  22.9 us
    another operation x1, loops' own time, on_device(): lax.switch(case_index, forward_cases, query_heads, key_heads, value_heads)  22.7 us
  transfers between devices with their start and end apart: 10, of which 2 were waited for; matrix products, arithmetic and copies ran while one was open for 11% of the time, Pallas kernels for 0%

commit v1 on v0

v1 whole, which is shorter than its diff:
```python
from functools import partial
import math
import jax
import jax.numpy as jnp
from jax import lax
from jax.experimental import pallas as pl
from jax.experimental.pallas import tpu as pltpu
from jax.sharding import PartitionSpec as P

BLOCK = 256
SLOT_OPTIONS = (1, 2, 4, 8)
LOG2E = math.log2(math.e)
F32, BF16 = jnp.float32, jnp.bfloat16
MASKED = -1e30
EPS = 1e-05
MIB = 1 << 20


def nn(a, b):
    return lax.dot_general(a, b, (((1,), (0,)), ((), ())), preferred_element_type=F32)


def nt(a, b):
    return lax.dot_general(a, b, (((1,), (1,)), ((), ())), preferred_element_type=F32)


def tn(a, b):
    return lax.dot_general(a, b, (((0,), (0,)), ((), ())), preferred_element_type=F32)


def sorter(count, transposed=False):
    each = BLOCK // count
    grouped = lax.broadcasted_iota(jnp.int32, (BLOCK, BLOCK), 1 if transposed else 0)
    plain = lax.broadcasted_iota(jnp.int32, (BLOCK, BLOCK), 0 if transposed else 1)
    place = (plain & (count - 1)) * each + (plain >> (count.bit_length() - 1))
    return jnp.where(grouped == place, 1.0, 0.0).astype(BF16)


def store_grouped(write, values, tile, total, count):
    each = BLOCK // count
    for group in range(count):
        start = pl.multiple_of(group * (total // count) + tile * each, each)
        write(pl.ds(start, each), values[group * each : (group + 1) * each])


def load_grouped(read, tile, total, count):
    each = BLOCK // count
    parts = []
    for group in range(count):
        start = pl.multiple_of(group * (total // count) + tile * each, each)
        parts.append(read(pl.ds(start, each)))
    return parts[0] if count == 1 else jnp.concatenate(parts, axis=0)


def normalized(rows):
    average = jnp.mean(rows, axis=-1, keepdims=True)
    centred = rows - average
    spread = jnp.mean(centred * centred, axis=-1, keepdims=True)
    scale = lax.rsqrt(spread + EPS)
    return centred * scale, scale


def as_columns(vectors):
    stack = jnp.concatenate(vectors + [jnp.zeros((128 - len(vectors), vectors[0].shape[1]), F32)], axis=0)
    return jnp.transpose(stack).astype(BF16)


def forward_kernel(
    info, own, other, skip_own, skip_other, query_weight, key_weight, value_weight, gain, shift,
    mixed_own, mixed_other, query, keys, saved, mixed, logsum, normed, values,
):
    count, head = info[0], info[1]
    half = own.shape[0]
    total = 2 * half
    blocks = total // BLOCK
    values[:, :, 128:] = jnp.ones((2, total, 128), BF16)

    for rows_ref, skip_ref, which in ((own, skip_own, head), (other, skip_other, 1 - head)):

        def project(step, _, rows_ref=rows_ref, skip_ref=skip_ref, which=which):
            at = pl.ds(pl.multiple_of(step * BLOCK, BLOCK), BLOCK)
            tile = which * (half // BLOCK) + step
            hat, _s = normalized(rows_ref[at, :].astype(F32))
            low = (hat * gain[...] + shift[...]).astype(BF16)
            skip = skip_ref[at, :]

            def put(count_here):
                rows, skipped = low, skip
                if count_here > 1:
                    order = sorter(count_here)
                    rows = nn(order, low).astype(BF16)
                    skipped = nn(order, skip).astype(BF16)
                q = nn(rows, query_weight[...]).astype(BF16)
                q = q * jnp.asarray(0.125, BF16)
                k = nn(rows, key_weight[...]).astype(BF16)
                f = nn(rows, value_weight[...]).astype(BF16)

                def put_in(ref, part, value):
                    def write(dst, piece):
                        if part is None:
                            ref[dst, :] = piece
                        else:
                            ref[part, dst, :128] = piece
                            if ref is values:
                                saved[part, dst, :] = piece

                    store_grouped(write, value, tile, total, count_here)

                put_in(normed, None, rows)
                put_in(query, 0, q[:, :128])
                put_in(query, 1, q[:, 128:])
                put_in(keys, 0, k[:, :128])
                put_in(keys, 1, k[:, 128:])
                put_in(values, 0, f)
                put_in(values, 1, skipped)

            for option in SLOT_OPTIONS:
                pl.when(count == option)(partial(put, option))
            return 0

        lax.fori_loop(0, half // BLOCK, project, 0)

    per_slot = blocks // count
    lane = lax.broadcasted_iota(jnp.int32, (1, 128), 1)
    tri = lax.broadcasted_iota(jnp.int32, (BLOCK, BLOCK), 1) <= lax.broadcasted_iota(
        jnp.int32, (BLOCK, BLOCK), 0
    )

    def attend(block, _):
        width = block % per_slot + 1
        here = pl.multiple_of(block * BLOCK, BLOCK)

        def run(wide):
            first = pl.multiple_of((block - (wide - 1)) * BLOCK, BLOCK)

            def score(h):
                pair, sub = h // 2, h % 2
                q = query[pair, pl.ds(here, BLOCK), :]
                qm = jnp.where((lane < 64) == (sub == 0), q, jnp.zeros_like(q))
                diag = nt(qm, keys[pair, pl.ds(here, BLOCK), :]) * LOG2E
                rest = None
                if wide > 1:
                    rest = nt(qm, keys[pair, pl.ds(first, (wide - 1) * BLOCK), :]) * LOG2E
                return diag, rest

            def finish(h, diag, rest):
                pair, sub = h // 2, h % 2
                diag = jnp.where(tri, diag, MASKED)
                top = jnp.max(diag, axis=1, keepdims=True)
                if wide > 1:
                    top = jnp.maximum(top, jnp.max(rest, axis=1, keepdims=True))
                raised = jnp.exp2(diag - top).astype(BF16)
                acc = nn(raised, values[pair, pl.ds(here, BLOCK), :])
                if wide > 1:
                    raised = jnp.exp2(rest - top).astype(BF16)
                    acc += nn(raised, values[pair, pl.ds(first, (wide - 1) * BLOCK), :])
                sums = acc[:, 128:]
                return acc[:, :128] / sums, jnp.transpose(top + jnp.log2(sums))[0:1, :]

            nxt = score(0)
            outs = []
            for h in range(4):
                cur = nxt
                if h < 3:
                    nxt = score(h + 1)
                outs.append(finish(h, *cur))
            for pair in range(2):
                mixed[pair, pl.ds(here, BLOCK), :] = jnp.where(lane < 64, outs[2*pair][0], outs[2*pair+1][0]).astype(BF16)
                for sub in range(2):
                    logsum[pair, sub : sub + 1, pl.ds(here, BLOCK)] = outs[2*pair+sub][1]

        for wide in range(1, blocks + 1):
            pl.when(width == wide)(partial(run, wide))
        return 0

    lax.fori_loop(0, blocks, attend, 0)

    for out_ref, which in ((mixed_own, head), (mixed_other, 1 - head)):

        def give(step, _, out_ref=out_ref, which=which):
            at = pl.ds(pl.multiple_of(step * BLOCK, BLOCK), BLOCK)
            tile = which * (half // BLOCK) + step

            def put(count_here):
                for pair in range(2):
                    part = load_grouped(lambda s: mixed[pair, s, :], tile, total, count_here)
                    if count_here > 1:
                        part = nn(sorter(count_here, True), part).astype(BF16)
                    out_ref[at, pair * 128 : (pair + 1) * 128] = part

            for option in SLOT_OPTIONS:
                pl.when(count == option)(partial(put, option))
            return 0

        lax.fori_loop(0, half // BLOCK, give, 0)


def whole(shape):
    return pl.BlockSpec(shape, lambda i, s: (0,) * len(shape))


def forward_attention(info, own, other, skip_own, skip_other, wq, wk, wv, gain, shift):
    half, width = own.shape
    total = 2 * half
    group = wq.shape[1] // 2
    outs = [
        ((half, group), BF16),
        ((half, group), BF16),
        ((2, total, 128), BF16),
        ((2, total, 128), BF16),
        ((2, total, 128), BF16),
        ((2, total, 128), BF16),
        ((2, 8, total), F32),
        ((total, width), BF16),
    ]
    return pl.pallas_call(
        forward_kernel,
        grid_spec=pltpu.PrefetchScalarGridSpec(
            num_scalar_prefetch=1,
            grid=(1,),
            in_specs=[
                whole(own.shape),
                whole(other.shape),
                pl.BlockSpec((half, 128), lambda i, s: (0, s[1])),
                whole(skip_other.shape),
                pl.BlockSpec((width, group), lambda i, s: (0, s[1])),
                pl.BlockSpec((width, group), lambda i, s: (0, s[1])),
                pl.BlockSpec((width, 128), lambda i, s: (0, s[1])),
                whole(gain.shape),
                whole(shift.shape),
            ],
            out_specs=[whole(s) for s, _ in outs],
            scratch_shapes=[pltpu.VMEM((2, total, 256), BF16)],
        ),
        out_shape=[jax.ShapeDtypeStruct(s, d) for s, d in outs],
        compiler_params=pltpu.CompilerParams(vmem_limit_bytes=56 * MIB),
        name="forward_attention",
    )(info, own, other, skip_own, skip_other, wq, wk, wv, gain, shift)


COLS = 512
GELU_SLOPE = math.sqrt(2.0 / math.pi)
GELU_CUBE = 0.044715


def gelu_pair(v):
    square = v * v
    bend = jnp.tanh(v * (GELU_SLOPE + (GELU_SLOPE * GELU_CUBE) * square))
    front = 0.5 + 0.5 * bend
    slope = front + (0.5 * v) * (1.0 - bend * bend) * (
        GELU_SLOPE + (3.0 * GELU_SLOPE * GELU_CUBE) * square
    )
    return v * front, slope


def rows_kernel(
    info, lengths, tokens, mixed_own, mixed_other, cotangent, mixing_weight, expand_weight,
    shrink_weight, expand_bias, gain, shift,
    output, after_grad, send_own, send_other, shrink_grad, wide_grad,
    bias_grad, gain_grads, active, slope, pre_grad, middle, out_grad, after_low,
):
    count, head = info[0], info[1]
    half, width = tokens.shape
    hidden = expand_weight.shape[1]
    group = mixed_own.shape[1]
    shift_by = (
        (count >= 2).astype(jnp.int32)
        + (count >= 4).astype(jnp.int32)
        + (count >= 8).astype(jnp.int32)
    )
    here = pl.ds(pl.multiple_of(head * group, group), group)
    there = pl.ds(pl.multiple_of((1 - head) * group, group), group)
    bias_grad[...] = jnp.zeros_like(bias_grad)
    gain_grads[...] = jnp.zeros_like(gain_grads)

    def tile(step, _):
        at = pl.ds(pl.multiple_of(step * BLOCK, BLOCK), BLOCK)
        row = head * half + step * BLOCK + lax.broadcasted_iota(jnp.int32, (BLOCK, 1), 0)
        slot = row & (count - 1)
        limit = jnp.zeros_like(row)
        for s in range(lengths.shape[0]):
            limit = jnp.where(slot == s, lengths[s], limit)
        valid = (row >> shift_by) < limit
        after = (
            tokens[at, :].astype(F32)
            + nn(mixed_own[at, :], mixing_weight[here, :])
            + nn(mixed_other[at, :], mixing_weight[there, :])
        )
        hat, scale = normalized(after)
        low = (hat * gain[...] + shift[...]).astype(BF16)
        middle[at, :] = low
        for c in range(0, hidden, COLS):
            cs = slice(c, c + COLS)
            act, slo = gelu_pair(nn(low, expand_weight[:, cs]) + expand_bias[:, cs])
            active[at, cs] = act.astype(BF16)
            slope[:, cs] = slo
        grown = nn(active[at, :], shrink_weight[...])
        output[at, :] = jnp.where(valid, after + grown, 0.0).astype(BF16)
        grad_out = jnp.where(valid, cotangent[at, :].astype(F32), 0.0)
        grad_low = grad_out.astype(BF16)
        out_grad[at, :] = grad_low
        for c in range(0, hidden, COLS):
            cs = slice(c, c + COLS)
            g = nt(grad_low, shrink_weight[cs, :]) * slope[:, cs]
            bias_grad[0:1, cs] += jnp.sum(g, axis=0, keepdims=True)
            pre_grad[at, cs] = g.astype(BF16)
        g_middle = nt(pre_grad[at, :], expand_weight[...])
        gain_grads[0:1, :] += jnp.sum(g_middle * hat, axis=0, keepdims=True)
        gain_grads[1:2, :] += jnp.sum(g_middle, axis=0, keepdims=True)
        y = g_middle * gain[...]
        g_after = grad_out + scale * (
            y
            - jnp.mean(y, axis=-1, keepdims=True)
            - hat * jnp.mean(y * hat, axis=-1, keepdims=True)
        )
        after_grad[at, :] = g_after
        g_low = g_after.astype(BF16)
        after_low[at, :] = g_low
        send_own[at, :] = nt(g_low, mixing_weight[here, :]).astype(BF16)
        send_other[at, :] = nt(g_low, mixing_weight[there, :]).astype(BF16)
        return 0

    lax.fori_loop(0, half // BLOCK, tile, 0)

    def weights(step, _):
        cs = pl.ds(pl.multiple_of(step * COLS, COLS), COLS)
        shrink_grad[cs, :] = tn(active[:, cs], out_grad[...]).astype(BF16)
        wide_grad[:, cs] = tn(middle[...], pre_grad[:, cs]).astype(BF16)
        return 0

    lax.fori_loop(0, hidden // COLS, weights, 0)
    mix = slice(hidden, hidden + width)
    wide_grad[here, mix] = tn(mixed_own[...], after_low[...]).astype(BF16)
    wide_grad[there, mix] = tn(mixed_other[...], after_low[...]).astype(BF16)
    vectors = [bias_grad[0:1, c : c + width] for c in range(0, hidden, width)]
    vectors += [gain_grads[0:1, :], gain_grads[1:2, :]]
    wide_grad[:, hidden + width :] = as_columns(vectors)


def row_part(info, lengths, tokens, mixed_own, mixed_other, cotangent, wo, we, ws, bias, gain, shift):
    half, width = tokens.shape
    hidden = we.shape[1]
    group = mixed_own.shape[1]
    outs = [
        ((half, width), BF16),
        ((half, width), F32),
        ((half, group), BF16),
        ((half, group), BF16),
        ((hidden, width), BF16),
        ((width, hidden + width + 128), BF16),
    ]
    args = (tokens, mixed_own, mixed_other, cotangent, wo, we, ws, bias, gain, shift)
    block = lambda shape: pl.BlockSpec(shape, lambda i, s, t: (0,) * len(shape))
    return pl.pallas_call(
        rows_kernel,
        grid_spec=pltpu.PrefetchScalarGridSpec(
            num_scalar_prefetch=2,
            grid=(1,),
            in_specs=[block(a.shape) for a in args],
            out_specs=[block(s) for s, _ in outs],
            scratch_shapes=[
                pltpu.VMEM((8, hidden), F32),
                pltpu.VMEM((8, width), F32),
                pltpu.VMEM((half, hidden), BF16),
                pltpu.VMEM((BLOCK, hidden), F32),
                pltpu.VMEM((half, hidden), BF16),
                pltpu.VMEM((half, width), BF16),
                pltpu.VMEM((half, width), BF16),
                pltpu.VMEM((half, width), BF16),
            ],
        ),
        out_shape=[jax.ShapeDtypeStruct(s, d) for s, d in outs],
        compiler_params=pltpu.CompilerParams(vmem_limit_bytes=60 * MIB),
        name="row_part",
    )(info, lengths, *args)


def backward_kernel(
    info, own, other, grad_own, grad_other, query, keys, values, mixed, logsum, normed,
    query_weight, key_weight, value_weight,
    weight_grad, back_own, back_other, skip_own, skip_other,
    gain_grads, grad, inner, query_total, packed, skipped, back,
):
    count, head = info[0], info[1]
    half = own.shape[0]
    total = 2 * half
    blocks = total // BLOCK
    query_total[...] = jnp.zeros_like(query_total)

    for rows_ref, which in ((grad_own, head), (grad_other, 1 - head)):

        def arrange(step, _, rows_ref=rows_ref, which=which):
            at = pl.ds(pl.multiple_of(step * BLOCK, BLOCK), BLOCK)
            tile = which * (half // BLOCK) + step
            rows = rows_ref[at, :]

            def put(count_here):
                value = rows
                if count_here > 1:
                    value = nn(sorter(count_here), rows).astype(BF16)
                for pair in range(2):

                    def write(dst, piece, pair=pair):
                        grad[pair, dst, :] = piece

                    store_grouped(
                        write, value[:, pair * 128 : (pair + 1) * 128], tile, total, count_here
                    )

            for option in SLOT_OPTIONS:
                pl.when(count == option)(partial(put, option))
            return 0

        lax.fori_loop(0, half // BLOCK, arrange, 0)

    def inners(block, _):
        at = pl.ds(pl.multiple_of(block * BLOCK, BLOCK), BLOCK)
        for pair in range(2):
            flipped = jnp.transpose(grad[pair, at, :].astype(F32) * mixed[pair, at, :].astype(F32))
            for sub in range(2):
                inner[pair, sub : sub + 1, at] = jnp.sum(
                    flipped[sub * 64 : (sub + 1) * 64], axis=0, keepdims=True
                )
        return 0

    lax.fori_loop(0, blocks, inners, 0)

    per_slot = blocks // count
    lane = lax.broadcasted_iota(jnp.int32, (1, 128), 1)
    tri = lax.broadcasted_iota(jnp.int32, (BLOCK, BLOCK), 0) <= lax.broadcasted_iota(
        jnp.int32, (BLOCK, BLOCK), 1
    )

    def attend(block, _):
        width = per_slot - block % per_slot
        here = pl.multiple_of(block * BLOCK, BLOCK)

        def run(wide):
            span = pl.ds(here, wide * BLOCK)
            at = pl.ds(here, BLOCK)

            def score(h):
                pair, sub = h // 2, h % 2
                pick = (lane < 64) == (sub == 0)
                k, v = keys[pair, at, :], values[pair, at, :]
                k = jnp.where(pick, k, jnp.zeros_like(k))
                v = jnp.where(pick, v, jnp.zeros_like(v))
                return k, nt(k, query[pair, span, :]), nt(v, grad[pair, span, :])

            def finish(h, k, raw, grad_probs):
                pair, sub = h // 2, h % 2
                probs = jnp.exp2(raw * LOG2E - logsum[pair, sub : sub + 1, span])
                diag = jnp.where(tri, probs[:, :BLOCK], 0.0)
                probs = diag if wide == 1 else jnp.concatenate([diag, probs[:, BLOCK:]], axis=1)
                grad_scores = (probs * (grad_probs - inner[pair, sub : sub + 1, span])).astype(BF16)
                grad_value = nn(probs.astype(BF16), grad[pair, span, :])
                grad_key = nn(grad_scores, query[pair, span, :])
                return grad_value, grad_key, tn(grad_scores, k)

            ahead = score(0)
            done = []
            for h in range(4):
                now = ahead
                if h < 3:
                    ahead = score(h + 1)
                done.append(finish(h, *now))
                if h % 2:
                    pair = h // 2
                    first, second = done[h - 1], done[h]
                    gv = jnp.where(lane < 64, first[0], second[0]).astype(BF16)
                    gk = jnp.where(lane < 64, first[1], second[1]).astype(BF16)
                    packed[at, 256 + pair * 128 : 256 + (pair + 1) * 128] = gk
                    if pair == 0:
                        packed[at, 512:] = gv
                    else:
                        skipped[at, :] = gv
                    query_total[pair, span, :] += first[2] + second[2]

        for wide in range(1, blocks + 1):
            pl.when(width == wide)(partial(run, wide))
        return 0

    lax.fori_loop(0, blocks, attend, 0)

    def close(block, _):
        at = pl.ds(pl.multiple_of(block * BLOCK, BLOCK), BLOCK)
        for pair in range(2):
            packed[at, pair * 128 : (pair + 1) * 128] = (query_total[pair, at, :] * 0.125).astype(BF16)
        back[at, :] = (
            nt(packed[at, :256], query_weight[...])
            + nt(packed[at, 256:512], key_weight[...])
            + nt(packed[at, 512:], value_weight[...])
        ).astype(BF16)
        return 0

    lax.fori_loop(0, blocks, close, 0)
    weight_grad[:, :640] = tn(normed[...], packed[...]).astype(BF16)
    gain_grads[...] = jnp.zeros_like(gain_grads)

    for rows_ref, back_ref, skip_ref, which in (
        (own, back_own, skip_own, head),
        (other, back_other, skip_other, 1 - head),
    ):

        def give(step, _, rows_ref=rows_ref, back_ref=back_ref, skip_ref=skip_ref, which=which):
            at = pl.ds(pl.multiple_of(step * BLOCK, BLOCK), BLOCK)
            tile = which * (half // BLOCK) + step

            def put(count_here):
                g = load_grouped(lambda s: back[s, :], tile, total, count_here)
                k = load_grouped(lambda s: skipped[s, :], tile, total, count_here)
                if count_here > 1:
                    order = sorter(count_here, True)
                    g = nn(order, g).astype(BF16)
                    k = nn(order, k).astype(BF16)
                back_ref[at, :] = g
                skip_ref[at, :] = k

            for option in SLOT_OPTIONS:
                pl.when(count == option)(partial(put, option))
            hat, _s = normalized(rows_ref[at, :].astype(F32))
            g = back_ref[at, :].astype(F32)
            gain_grads[0:1, :] += jnp.sum(g * hat, axis=0, keepdims=True)
            gain_grads[1:2, :] += jnp.sum(g, axis=0, keepdims=True)
            return 0

        lax.fori_loop(0, half // BLOCK, give, 0)
    weight_grad[:, 640:] = as_columns([gain_grads[0:1, :], gain_grads[1:2, :]])


def backward_attention(
    info, own, other, grad_own, grad_other, query, keys, values, mixed, logsum, normed, wq, wk, wv
):
    half, width = own.shape
    total = 2 * half
    group = wq.shape[1] // 2
    outs = [
        ((width, 768), BF16),
        ((half, width), BF16),
        ((half, width), BF16),
        ((half, 128), BF16),
        ((half, 128), BF16),
    ]
    args = (own, other, grad_own, grad_other, query, keys, values, mixed, logsum, normed)
    return pl.pallas_call(
        backward_kernel,
        grid_spec=pltpu.PrefetchScalarGridSpec(
            num_scalar_prefetch=1,
            grid=(1,),
            in_specs=[whole(a.shape) for a in args]
            + [
                pl.BlockSpec((width, group), lambda i, s: (0, s[1])),
                pl.BlockSpec((width, group), lambda i, s: (0, s[1])),
                pl.BlockSpec((width, 128), lambda i, s: (0, s[1])),
            ],
            out_specs=[whole(s) for s, _ in outs],
            scratch_shapes=[
                pltpu.VMEM((8, width), F32),
                pltpu.VMEM((2, total, 128), BF16),
                pltpu.VMEM((2, 8, total), F32),
                pltpu.VMEM((2, total, 128), F32),
                pltpu.VMEM((total, 640), BF16),
                pltpu.VMEM((total, 128), BF16),
                pltpu.VMEM((total, width), BF16),
            ],
        ),
        out_shape=[jax.ShapeDtypeStruct(s, d) for s, d in outs],
        compiler_params=pltpu.CompilerParams(vmem_limit_bytes=60 * MIB),
        name="backward_attention",
    )(info, *args, wq, wk, wv)


def close_kernel(info, tokens, after_grad, back_own, back_other, gain, kept, arrived, result, skip_grad):
    head = info[1]

    def tile(step, _):
        at = pl.ds(pl.multiple_of(step * BLOCK, BLOCK), BLOCK)
        hat, scale = normalized(tokens[at, :].astype(F32))
        y = (back_own[at, :].astype(F32) + back_other[at, :].astype(F32)) * gain[...]
        result[at, :] = (
            after_grad[at, :]
            + scale
            * (
                y
                - jnp.mean(y, axis=-1, keepdims=True)
                - hat * jnp.mean(y * hat, axis=-1, keepdims=True)
            )
        ).astype(BF16)
        return 0

    lax.fori_loop(0, tokens.shape[0] // BLOCK, tile, 0)
    skip_grad[:, pl.ds(pl.multiple_of(head * 128, 128), 128)] = kept[...]
    skip_grad[:, pl.ds(pl.multiple_of((1 - head) * 128, 128), 128)] = arrived[...]


def close_rows(info, tokens, after_grad, back_own, back_other, gain, kept, arrived):
    args = (tokens, after_grad, back_own, back_other, gain, kept, arrived)
    half = tokens.shape[0]
    return pl.pallas_call(
        close_kernel,
        grid_spec=pltpu.PrefetchScalarGridSpec(
            num_scalar_prefetch=1,
            grid=(1,),
            in_specs=[whole(a.shape) for a in args],
            out_specs=[whole(tokens.shape), whole((half, 256))],
        ),
        out_shape=[
            jax.ShapeDtypeStruct(tokens.shape, BF16),
            jax.ShapeDtypeStruct((half, 256), BF16),
        ],
        compiler_params=pltpu.CompilerParams(vmem_limit_bytes=32 * MIB),
        name="close_rows",
    )(info, *args)


def swap_cores(array):
    return lax.ppermute(array, "head", [(0, 1), (1, 0)])


def half_of(array, which):
    rows = array.shape[0] // 2
    return lax.dynamic_slice_in_dim(array, which * rows, rows, 0)


def add_low(a, b):
    return (a.astype(F32) + b.astype(F32)).astype(BF16)


def swap_bit(array, bit):
    size = lax.axis_size("seq")
    return lax.ppermute(array, "seq", [(i, i ^ (1 << bit)) for i in range(size)])


def bit_of(bit):
    return (lax.axis_index("seq") >> bit) & 1


def join(mine, theirs, which):
    both = jnp.concatenate([mine, mine], axis=0)
    return lax.dynamic_update_slice_in_dim(both, theirs, (1 - which) * mine.shape[0], 0)


def seq_sum(chunks, first_bits):
    bits = lax.axis_size("seq").bit_length() - 1
    orders = [[(f + s) % min(3, bits) for s in range(min(3, bits))] + list(range(3, bits)) for f in first_bits]
    trail = [[] for _ in chunks]
    for stage in range(bits):
        after = []
        for chunk, order, path in zip(chunks, orders, trail):
            bit = order[stage]
            if chunk.shape[0] % 32 == 0:
                mine = bit_of(bit)
                path.append(bit)
                after.append(add_low(half_of(chunk, mine), swap_bit(half_of(chunk, 1 - mine), bit)))
            else:
                after.append(add_low(chunk, swap_bit(chunk, bit)))
        chunks = after
    while any(trail):
        for n, path in enumerate(trail):
            if path:
                bit = path.pop()
                chunks[n] = join(chunks[n], swap_bit(chunks[n], bit), bit_of(bit))
    return chunks


def on_device(
    tokens, first_values, cotangent, slot_count, seq_lengths, query_weight, key_weight, value_weight,
    mixing_weight, expand_weight, shrink_weight, expand_bias, before_gain, before_shift,
    middle_gain, middle_shift,
):
    head = lax.axis_index("head")
    info = jnp.stack([slot_count[0], head.astype(jnp.int32)])
    lengths = seq_lengths[0]
    row = lambda v: v.reshape(1, -1)

    other = swap_cores(tokens)
    skip_other = swap_cores(lax.dynamic_slice_in_dim(first_values, (1 - head) * 128, 128, 1))
    mixed_own, mixed_away, query, keys, values, mixed, logsum, normed = forward_attention(
        info, tokens, other, first_values, skip_other, query_weight, key_weight, value_weight,
        row(before_gain), row(before_shift),
    )
    mixed_other = swap_cores(mixed_away)
    output, after_grad, grad_own, grad_away, shrink_part, wide_part = row_part(
        info, lengths, tokens, mixed_own, mixed_other, cotangent, mixing_weight, expand_weight,
        shrink_weight, row(expand_bias), row(middle_gain), row(middle_shift),
    )
    grad_other = swap_cores(grad_away)
    shrink_half = add_low(half_of(shrink_part, head), swap_cores(half_of(shrink_part, 1 - head)))
    wide_half = add_low(half_of(wide_part, head), swap_cores(half_of(wide_part, 1 - head)))
    shrink_half, wide_half = seq_sum([shrink_half, wide_half], (0, 1))

    projection_part, back_own, back_away, skip_own, skip_away = backward_attention(
        info, tokens, other, grad_own, grad_other, query, keys, values, mixed, logsum, normed,
        query_weight, key_weight, value_weight,
    )
    back_other = swap_cores(back_away)
    skip_arrived = swap_cores(skip_away)
    (projection,) = seq_sum([projection_part], (0,))
    input_grad, skip_grad = close_rows(
        info, tokens, after_grad, back_own, back_other, row(before_gain), skip_own, skip_arrived
    )
    shrink_grad = join(shrink_half, swap_cores(shrink_half), head).astype(F32)
    wide = join(wide_half, swap_cores(wide_half), head)
    hidden, width = shrink_grad.shape
    expand_grad = wide[:, :hidden].astype(F32)
    mixing_grad = wide[:, hidden : hidden + width].astype(F32)
    tail = wide[:, hidden + width : hidden + width + 8].astype(F32)
    bias_grad = tail[:, : hidden // width].T.reshape(hidden)
    middle_gain_grad, middle_shift_grad = tail[:, 4], tail[:, 5]
    arrived = swap_cores(projection)
    low_head = jnp.where(head == 0, projection, arrived).astype(F32)
    high_head = jnp.where(head == 0, arrived, projection).astype(F32)
    query_grad = jnp.concatenate([low_head[:, :256], high_head[:, :256]], axis=1)
    key_grad = jnp.concatenate([low_head[:, 256:512], high_head[:, 256:512]], axis=1)
    value_grad = jnp.concatenate([low_head[:, 512:640], high_head[:, 512:640]], axis=1)
    edges = low_head[:, 640:642] + high_head[:, 640:642]
    return (
        output, input_grad, skip_grad, query_grad, key_grad, value_grad, mixing_grad, expand_grad,
        shrink_grad, bias_grad, edges[:, 0], edges[:, 1], middle_gain_grad, middle_shift_grad,
    )


def solution(mesh):
    rows = P(("seq", "head"), None)
    return jax.shard_map(
        on_device,
        mesh=mesh,
        in_specs=(rows, rows, rows, P("seq"), P("seq", None)) + (P(),) * 11,
        out_specs=(rows, rows, rows) + (P(),) * 11,
        check_vma=False,
    )
```

time: 628 us -> 258 us (0.41)
  matrix products: 157 us -> 0 us
  Pallas kernels: 0 us -> 108 us
  waiting for transfers between devices: 163 us -> 95.7 us
  local copies, waits for them, and re-layouts: 72.9 us -> 10.7 us
  blocking collectives: 58.4 us -> 0 us
  loops' own time: 50.6 us -> 0 us
  other arithmetic: 63.7 us -> 13.5 us
  starting transfers between devices: 39.4 us -> 24.6 us
  between operations: 15.8 us -> 2.12 us
    psum x1 -> x0, waiting for transfers between devices: 162 us -> none  [on_device(): lax.psum((gradients[0], gradients[1], gradients[2], gradients[3], gradien...]
    dot_general x47 -> x0, matrix products: 157 us -> none  [the longest x6 24.5 us: left_matmul(): lax.dot_general(left_side, right_side, (((0,), (0,)), ((), ())), preferre...]
    pallas_call x0 -> x4, Pallas kernels: none -> 108 us  [the longest x1 51.4 us: backward_attention(): pl.pallas_call(backward_kernel, grid_spec=pltpu.PrefetchScalarGridSpec(nu...]
    ppermute x0 -> x35, waiting for transfers between devices: none -> 95.7 us  [the longest x24 91.8 us: swap_bit(): return lax.ppermute(array, 'seq', [(i, i ^ 1 << bit) for i in range(size)])]
    psum x1 -> x0, blocking collectives: 53 us -> none  [on_device(): lax.psum((gradients[0], gradients[1], gradients[2], gradients[3], gradien...]
    another operation x2 -> x0, loops' own time: 50.6 us -> none  [the longest x1 27.9 us: on_device(): lax.switch(case_index, backward_cases, query_heads, key_heads, value_head...]
    all_to_all x9 -> x0, starting transfers between devices: 39.4 us -> none  [the longest x1 4.57 us: on_device(): lax.all_to_all(shortened(mixed_heads), 'head', split_axis=0, concat_axis=...]
    unnamed x116 -> x31, local copies, waits for them, and re-layouts: 28.7 us -> 3.31 us
  transfers between devices with their start and end apart: 10 -> 35, of which waited for: 2 -> 20; matrix products, arithmetic and copies ran while one was open for 11% -> 6% of each run, Pallas kernels for 0% -> 1%
where the time goes in v1:
time: 258 us; the launch traced here: 255 us
  Pallas kernels  108 us (42%)
  waiting for transfers between devices  95.7 us (37%)
  starting transfers between devices  24.6 us (10%)
  other arithmetic  13.5 us (5%)
  local copies, waits for them, and re-layouts  10.7 us (4%)
    ppermute x24, waiting for transfers between devices, swap_bit(): return lax.ppermute(array, 'seq', [(i, i ^ 1 << bit) for i in range(size)])  91.8 us
    pallas_call x1, Pallas kernels, backward_attention(): pl.pallas_call(backward_kernel, grid_spec=pltpu.PrefetchScalarGridSpec(nu...  51.4 us
    pallas_call x1, Pallas kernels, forward_attention(): pl.pallas_call(forward_kernel, grid_spec=pltpu.PrefetchScalarGridSpec(num...  26.9 us
    pallas_call x1, Pallas kernels, row_part(): pl.pallas_call(rows_kernel, grid_spec=pltpu.PrefetchScalarGridSpec(num_sc...  26.4 us
    ppermute x24, starting transfers between devices, swap_bit(): return lax.ppermute(array, 'seq', [(i, i ^ 1 << bit) for i in range(size)])  21.5 us
  transfers between devices with their start and end apart: 35, of which 20 were waited for; matrix products, arithmetic and copies ran while one was open for 6% of the time, Pallas kernels for 1%

profile of v1, /device:TPU:0, one launch (start us, length us, event | category | flops | bytes accessed | tf_op | source)
XLA Modules:
  0.0 254.6 jit_solution(2940072130939483753)
XLA Ops:
  4.9 26.9 %forward_attention.1 = (bf16[1024,256]{1,0:T(8,128)(2,1)}, bf16[1024,256]{1,0:T(8,128)(2,1)}, bf16[2,2048,128]{2,1,0:T(8,128)(2,1)}, bf16[2,2048,128]{2,1,0:T(8,...) custom-call(s32[2]{0:T(128)} %pad_add_fusion.info, ...), custom_call_target="tpu_custom_call" | custom-call | tf_op jit(solution)/shard_map/forward_attention/pallas_call | solution.py:216
  32.2 1.7 collective-permute-done.2.mixed_other
  34.7 26.4 %row_part.1 = (bf16[1024,512]{1,0:T(8,128)(2,1)}, f32[1024,512]{1,0:T(8,128)}, bf16[1024,256]{1,0:T(8,128)(2,1)}, bf16[1024,256]{1,0:T(8,128)(2,1)}, bf16[2048,5...) custom-call(s32[2]{0:T(128)} %pad_add_fusion.info, s32[8]{0:T(128)} %bitcast.19, bf16[1024,512]{1,0:T(8,128)(2,1)} %tokens.3, ...), custom_call_target="tpu_custom_call" | custom-call | tf_op jit(solution)/shard_map/row_part/pallas_call | solution.py:354
  61.5 1.7 collective-permute-done.3.grad_other
  64.0 51.4 %backward_attention.1 = (bf16[512,768]{1,0:T(8,128)(2,1)}, bf16[1024,512]{1,0:T(8,128)(2,1)}, bf16[1024,512]{1,0:T(8,128)(2,1)}, bf16[1024,128]{1,0:T(8,128)(2,1)}, bf16[1024,128]{1,0:T(8,128)(2,1)}) custom-call(s32[2]{0:T(128)} %pad_add_fusion.info, bf16[1024,512]{1,0:T(8,128)(2,1)} %tokens.3, bf16[1024,512]{1,0:T(8,128)(2,1)} %copy-done.6, ...), custom_call_target="tpu_custom_call" | custom-call | tf_op jit(solution)/shard_map/backward_attention/pallas_call | solution.py:545
  115.4 1.8 constant_dynamic-slice_fusion.13
  119.1 9.8 %collective-permute-done.6 = bf16[256,768]{1,0:T(8,128)(2,1)} collective-permute-done((bf16[256,768]{1,0:T(8,128)(2,1)}, bf16[256,768]{1,0:T(8,128)(2,1)}, u32[]{:S(2)}, u32[]{:S(2)}) %collective-permute-start.6) | collective-permute-done | bytes 393248 | tf_op jit(solution)/shard_map/ppermute | solution.py:631
  130.9 5.5 %collective-permute-done.7 = bf16[128,768]{1,0:T(8,128)(2,1)S(1)} collective-permute-done((bf16[128,768]{1,0:T(8,128)(2,1)S(1)}, bf16[128,768]{1,0:T(8,128)(2,1)S(1)}, u32[]{:S(2)}, u32[]{:S(2)}) %collective-permute-start.7) | collective-permute-done | bytes 196640 | tf_op jit(solution)/shard_map/ppermute | solution.py:631
  136.5 2.3 collective-permute-start.8
  139.1 2.3 collective-permute-done.8
  142.3 4.2 %collective-permute-done.9 = bf16[32,768]{1,0:T(8,128)(2,1)S(1)} collective-permute-done((bf16[32,768]{1,0:T(8,128)(2,1)S(1)}, bf16[32,768]{1,0:T(8,128)(2,1)S(1)}, u32[]{:S(2)}, u32[]{:S(2)}) %collective-permute-start.9) | collective-permute-done | bytes 49184 | tf_op jit(solution)/shard_map/ppermute | solution.py:631
  146.6 5.1 %collective-permute-done.10 = bf16[32,768]{1,0:T(8,128)(2,1)S(1)} collective-permute-done((bf16[32,768]{1,0:T(8,128)(2,1)S(1)}, bf16[32,768]{1,0:T(8,128)(2,1)S(1)}, u32[]{:S(2)}, u32[]{:S(2)}) %collective-permute-start.10) | collective-permute-done | bytes 49184 | tf_op jit(solution)/shard_map/ppermute | solution.py:631
  151.7 2.6 %collective-permute-start.11 = (bf16[64,768]{1,0:T(8,128)(2,1)S(1)}, bf16[64,768]{1,0:T(8,128)(2,1)S(1)}, u32[]{:S(2)}, u32[]{:S(2)}) collective-permute-start(bf16[64,768]{1,0:T(8,128)(2,1)S(1)} %constant_dynamic-update-slice_fusion.13), channel_id=1, source_target_pairs={{0,8},{2,10},{4,12},{6,14},{8,0},{10,2},{12,4},{14,6},{16,24},{18,... | collective-permute-start | bytes 294920 | tf_op jit(solution)/shard_map/ppermute | solution.py:631
  155.0 1.5 collective-permute-start.27
  157.2 1.5 collective-permute-start.12
  158.7 5.6 %collective-permute-done.27 = bf16[256,512]{1,0:T(8,128)(2,1)S(1)} collective-permute-done((bf16[256,512]{1,0:T(8,128)(2,1)S(1)}, bf16[256,512]{1,0:T(8,128)(2,1)S(1)}, u32[]{:S(2)}, u32[]{:S(2)}) %collective-permute-start.27) | collective-permute-done | bytes 262176 | tf_op jit(solution)/shard_map/ppermute | solution.py:631
  164.8 3.2 %close_rows.1 = (bf16[1024,512]{1,0:T(8,128)(2,1)}, bf16[1024,256]{1,0:T(8,128)(2,1)}) custom-call(s32[2]{0:T(128)S(1)} %copy-done.5, bf16[1024,512]{1,0:T(8,128)(2,1)S(1)} %copy-done, f32[1024,512]{1,0:T(8,128)S(1)} %copy-done.1, bf16[1024,512]{1,0:T(8,128)(2,1)S(1)} %copy-done.2, bf16[1024,512]{1,0:T(8,128)(2,1)S(1)} %collective-permute-done.4.back_other, ...), custom_call_target="tpu_custom_call" | custom-call | tf_op jit(solution)/shard_map/close_rows/pallas_call | solution.py:599
  168.0 9.5 %collective-permute-done.12 = bf16[128,768]{1,0:T(8,128)(2,1)S(1)} collective-permute-done((bf16[128,768]{1,0:T(8,128)(2,1)S(1)}, bf16[128,768]{1,0:T(8,128)(2,1)S(1)}, u32[]{:S(2)}, u32[]{:S(2)}) %collective-permute-start.12) | collective-permute-done | bytes 196640 | tf_op jit(solution)/shard_map/ppermute | solution.py:631
  178.9 2.4 collective-permute-start.29
  181.4 3.7 %collective-permute-done.29 = bf16[64,512]{1,0:T(8,128)(2,1)S(1)} collective-permute-done((bf16[64,512]{1,0:T(8,128)(2,1)S(1)}, bf16[64,512]{1,0:T(8,128)(2,1)S(1)}, u32[]{:S(2)}, u32[]{:S(2)}) %collective-permute-start.29) | collective-permute-done | bytes 65568 | tf_op jit(solution)/shard_map/ppermute | solution.py:631
  185.2 2.2 collective-permute-start.30
  188.1 2.9 %collective-permute-done.30 = bf16[64,512]{1,0:T(8,128)(2,1)S(1)} collective-permute-done((bf16[64,512]{1,0:T(8,128)(2,1)S(1)}, bf16[64,512]{1,0:T(8,128)(2,1)S(1)}, u32[]{:S(2)}, u32[]{:S(2)}) %collective-permute-start.30) | collective-permute-done | bytes 65568 | tf_op jit(solution)/shard_map/ppermute | solution.py:631
  191.3 5.0 %collective-permute-done.31 = bf16[128,512]{1,0:T(8,128)(2,1)S(1)} collective-permute-done((bf16[128,512]{1,0:T(8,128)(2,1)S(1)}, bf16[128,512]{1,0:T(8,128)(2,1)S(1)}, u32[]{:S(2)}, u32[]{:S(2)}) %collective-permute-start.31) | collective-permute-done | bytes 131104 | tf_op jit(solution)/shard_map/ppermute | solution.py:631
  198.4 4.3 %collective-permute-done.32 = bf16[256,512]{1,0:T(8,128)(2,1)S(1)} collective-permute-done((bf16[256,512]{1,0:T(8,128)(2,1)S(1)}, bf16[256,512]{1,0:T(8,128)(2,1)S(1)}, u32[]{:S(2)}, u32[]{:S(2)}) %collective-permute-start.32) | collective-permute-done | bytes 262176 | tf_op jit(solution)/shard_map/ppermute | solution.py:631
  203.6 1.5 collective-permute-done.18
  206.5 5.1 %collective-permute-done.19 = bf16[16,2688]{1,0:T(8,128)(2,1)S(1)} collective-permute-done((bf16[16,2688]{1,0:T(8,128)(2,1)S(1)}, bf16[16,2688]{1,0:T(8,128)(2,1)S(1)}, u32[]{:S(2)}, u32[]{:S(2)}) %collective-permute-start.19) | collective-permute-done | bytes 86048 | tf_op jit(solution)/shard_map/ppermute | solution.py:631
  212.0 5.2 %collective-permute-done.20 = bf16[16,2688]{1,0:T(8,128)(2,1)S(1)} collective-permute-done((bf16[16,2688]{1,0:T(8,128)(2,1)S(1)}, bf16[16,2688]{1,0:T(8,128)(2,1)S(1)}, u32[]{:S(2)}, u32[]{:S(2)}) %collective-permute-start.20) | collective-permute-done | bytes 86048 | tf_op jit(solution)/shard_map/ppermute | solution.py:631
  217.6 5.1 %collective-permute-done.21 = bf16[32,2688]{1,0:T(8,128)(2,1)S(1)} collective-permute-done((bf16[32,2688]{1,0:T(8,128)(2,1)S(1)}, bf16[32,2688]{1,0:T(8,128)(2,1)S(1)}, u32[]{:S(2)}, u32[]{:S(2)}) %collective-permute-start.21) | collective-permute-done | bytes 172064 | tf_op jit(solution)/shard_map/ppermute | solution.py:631
  222.8 7.2 %collective-permute-done.22 = bf16[64,2688]{1,0:T(8,128)(2,1)S(1)} collective-permute-done((bf16[64,2688]{1,0:T(8,128)(2,1)S(1)}, bf16[64,2688]{1,0:T(8,128)(2,1)S(1)}, u32[]{:S(2)}, u32[]{:S(2)}) %collective-permute-start.22) | collective-permute-done | bytes 344096 | tf_op jit(solution)/shard_map/ppermute | solution.py:631
  231.0 10.0 %collective-permute-done.23 = bf16[128,2688]{1,0:T(8,128)(2,1)S(1)} collective-permute-done((bf16[128,2688]{1,0:T(8,128)(2,1)S(1)}, bf16[128,2688]{1,0:T(8,128)(2,1)S(1)}, u32[]{:S(2)}, u32[]{:S(2)}) %collective-permute-start.23) | collective-permute-done | bytes 688160 | tf_op jit(solution)/shard_map/ppermute | solution.py:631
  246.2 2.6 %convert_element_type.190 = f32[2048,512]{1,0:T(8,128)} convert(bf16[2048,512]{1,0:T(8,128)(2,1)S(1)} %constant_dynamic-update-slice_fusion) | non-fusion elementwise | flops 1048576 | bytes 6291456 | tf_op jit(solution)/shard_map/convert_element_type | solution.py:702
  251.1 2.6 %slice_convert_fusion = f32[512,2048]{1,0:T(8,128)} fusion(bf16[512,2688]{1,0:T(8,128)(2,1)S(1)} %constant_dynamic-update-slice_fusion.5), kind=kLoop, calls=%fused_computation.2 | loop fusion | flops 1048576 | bytes 6291456 | tf_op jit(solution)/shard_map/convert_element_type | solution.py:705
  (147 shorter events, 29.7 us)
Async XLA Ops:
  0.6 3.2 %collective-permute-start = (bf16[1024,512]{1,0:T(8,128)(2,1)}, bf16[1024,512]{1,0:T(8,128)(2,1)S(1)}, u32[]{:S(2)}, u32[]{:S(2)}) collective-permute-start(bf16[1024,512]{1,0:T(8,128)(2,1)} %tokens.3), channel_id=1, source_target_pairs={{0,1},{1,0},{2,3},{3,2},{4,5},{5,4},{6,7},{7,6},{8,9},{9,8},{10,11... | collective-permute-start | bytes 3145736 | tf_op jit(solution)/shard_map/ppermute | solution.py:617
  117.2 11.7 %collective-permute-start.6 = (bf16[256,768]{1,0:T(8,128)(2,1)}, bf16[256,768]{1,0:T(8,128)(2,1)}, u32[]{:S(2)}, u32[]{:S(2)}) collective-permute-start(bf16[256,768]{1,0:T(8,128)(2,1)} %constant_dynamic-slice_fusion.13), channel_id=1, source_target_pairs={{0,2},{2,0},{4,6},{6,4},{8,10},{10,8},{12,14},{14,12},{16,18},{18,... | collective-permute-start | bytes 1179656 | tf_op jit(solution)/shard_map/ppermute | solution.py:631
  118.7 20.1 %collective-permute-start.25 = (bf16[1024,512]{1,0:T(8,128)(2,1)S(1)}, bf16[1024,512]{1,0:T(8,128)(2,1)S(1)}, u32[]{:S(2)}, u32[]{:S(2)}) collective-permute-start(bf16[1024,512]{1,0:T(8,128)(2,1)S(1)} %constant_dynamic-slice_fusion.4), channel_id=1, source_target_pairs={{0,1},{1,0},{2,3},{3,2},{4,5},{5,4},{6,7},{7,6},{8,9},{9,8},{10,11... | collective-permute-start | bytes 3145736 | tf_op jit(solution)/shard_map/ppermute | solution.py:617
  130.0 6.4 %collective-permute-start.7 = (bf16[128,768]{1,0:T(8,128)(2,1)S(1)}, bf16[128,768]{1,0:T(8,128)(2,1)S(1)}, u32[]{:S(2)}, u32[]{:S(2)}) collective-permute-start(bf16[128,768]{1,0:T(8,128)(2,1)S(1)} %constant_dynamic-slice_fusion.12), channel_id=1, source_target_pairs={{0,4},{2,6},{4,0},{6,2},{8,12},{10,14},{12,8},{14,10},{16,20},{18,... | collective-permute-start | bytes 589832 | tf_op jit(solution)/shard_map/ppermute | solution.py:631
  130.2 24.1 %collective-permute-start.15 = (bf16[256,2688]{1,0:T(8,128)(2,1)S(1)}, bf16[256,2688]{1,0:T(8,128)(2,1)S(1)}, u32[]{:S(2)}, u32[]{:S(2)}) collective-permute-start(bf16[256,2688]{1,0:T(8,128)(2,1)S(1)} %constant_dynamic-slice_fusion.9), channel_id=1, source_target_pairs={{0,1},{1,0},{2,3},{3,2},{4,5},{5,4},{6,7},{7,6},{8,9},{9,8},{10,11... | collective-permute-start | bytes 4128776 | tf_op jit(solution)/shard_map/ppermute | solution.py:617
  130.3 34.4 %collective-permute-start.5 = (bf16[1024,128]{1,0:T(8,128)(2,1)S(1)}, bf16[1024,128]{1,0:T(8,128)(2,1)S(1)}, u32[]{:S(2)}, u32[]{:S(2)}) collective-permute-start(bf16[1024,128]{1,0:T(8,128)(2,1)S(1)} %copy-done.14), channel_id=1, source_target_pairs={{0,1},{1,0},{2,3},{3,2},{4,5},{5,4},{6,7},{7,6},{8,9},{9,8},{10,11... | collective-permute-start | bytes 786440 | tf_op jit(solution)/shard_map/ppermute | solution.py:617
  130.8 33.9 %collective-permute-start.4 = (bf16[1024,512]{1,0:T(8,128)(2,1)S(1)}, bf16[1024,512]{1,0:T(8,128)(2,1)S(1)}, u32[]{:S(2)}, u32[]{:S(2)}) collective-permute-start(bf16[1024,512]{1,0:T(8,128)(2,1)S(1)} %copy-done.13), channel_id=1, source_target_pairs={{0,1},{1,0},{2,3},{3,2},{4,5},{5,4},{6,7},{7,6},{8,9},{9,8},{10,11... | collective-permute-start | bytes 3145736 | tf_op jit(solution)/shard_map/ppermute | solution.py:617
  136.5 4.9 %collective-permute-start.8 = (bf16[64,768]{1,0:T(8,128)(2,1)S(1)}, bf16[64,768]{1,0:T(8,128)(2,1)S(1)}, u32[]{:S(2)}, u32[]{:S(2)}) collective-permute-start(bf16[64,768]{1,0:T(8,128)(2,1)S(1)} %constant_dynamic-slice_fusion.11), channel_id=1, source_target_pairs={{0,8},{2,10},{4,12},{6,14},{8,0},{10,2},{12,4},{14,6},{16,24},{18,... | collective-permute-start | bytes 294920 | tf_op jit(solution)/shard_map/ppermute | solution.py:631
  141.5 5.1 %collective-permute-start.9 = (bf16[32,768]{1,0:T(8,128)(2,1)S(1)}, bf16[32,768]{1,0:T(8,128)(2,1)S(1)}, u32[]{:S(2)}, u32[]{:S(2)}) collective-permute-start(bf16[32,768]{1,0:T(8,128)(2,1)S(1)} %constant_dynamic-slice_fusion.10), channel_id=1, source_target_pairs={{0,16},{2,18},{4,20},{6,22},{8,24},{10,26},{12,28},{14,30},{16,0},... | collective-permute-start | bytes 147464 | tf_op jit(solution)/shard_map/ppermute | solution.py:631
  141.6 13.2 %collective-permute-start.26 = (bf16[512,512]{1,0:T(8,128)(2,1)S(1)}, bf16[512,512]{1,0:T(8,128)(2,1)S(1)}, u32[]{:S(2)}, u32[]{:S(2)}) collective-permute-start(bf16[512,512]{1,0:T(8,128)(2,1)S(1)} %constant_dynamic-slice_fusion.3), channel_id=1, source_target_pairs={{0,2},{2,0},{4,6},{6,4},{8,10},{10,8},{12,14},{14,12},{16,18},{18,... | collective-permute-start | bytes 1572872 | tf_op jit(solution)/shard_map/ppermute | solution.py:631
  146.5 5.2 %collective-permute-start.10 = (bf16[32,768]{1,0:T(8,128)(2,1)S(1)}, bf16[32,768]{1,0:T(8,128)(2,1)S(1)}, u32[]{:S(2)}, u32[]{:S(2)}) collective-permute-start(bf16[32,768]{1,0:T(8,128)(2,1)S(1)} %add_convert_fusion.13), channel_id=1, source_target_pairs={{0,16},{2,18},{4,20},{6,22},{8,24},{10,26},{12,28},{14,30},{16,0},... | collective-permute-start | bytes 147464 | tf_op jit(solution)/shard_map/ppermute | solution.py:631
  151.7 5.5 %collective-permute-start.11 = (bf16[64,768]{1,0:T(8,128)(2,1)S(1)}, bf16[64,768]{1,0:T(8,128)(2,1)S(1)}, u32[]{:S(2)}, u32[]{:S(2)}) collective-permute-start(bf16[64,768]{1,0:T(8,128)(2,1)S(1)} %constant_dynamic-update-slice_fusion.13), channel_id=1, source_target_pairs={{0,8},{2,10},{4,12},{6,14},{8,0},{10,2},{12,4},{14,6},{16,24},{18,... | collective-permute-start | bytes 294920 | tf_op jit(solution)/shard_map/ppermute | solution.py:631
  155.0 9.3 %collective-permute-start.27 = (bf16[256,512]{1,0:T(8,128)(2,1)S(1)}, bf16[256,512]{1,0:T(8,128)(2,1)S(1)}, u32[]{:S(2)}, u32[]{:S(2)}) collective-permute-start(bf16[256,512]{1,0:T(8,128)(2,1)S(1)} %constant_dynamic-slice_fusion.2), channel_id=1, source_target_pairs={{0,4},{2,6},{4,0},{6,2},{8,12},{10,14},{12,8},{14,10},{16,20},{18,... | collective-permute-start | bytes 786440 | tf_op jit(solution)/shard_map/ppermute | solution.py:631
  156.6 30.8 %collective-permute-start.16 = (bf16[128,2688]{1,0:T(8,128)(2,1)S(1)}, bf16[128,2688]{1,0:T(8,128)(2,1)S(1)}, u32[]{:S(2)}, u32[]{:S(2)}) collective-permute-start(bf16[128,2688]{1,0:T(8,128)(2,1)S(1)} %constant_dynamic-slice_fusion.8), channel_id=1, source_target_pairs={{0,4},{2,6},{4,0},{6,2},{8,12},{10,14},{12,8},{14,10},{16,20},{18,... | collective-permute-start | bytes 2064392 | tf_op jit(solution)/shard_map/ppermute | solution.py:631
  157.2 20.3 %collective-permute-start.12 = (bf16[128,768]{1,0:T(8,128)(2,1)S(1)}, bf16[128,768]{1,0:T(8,128)(2,1)S(1)}, u32[]{:S(2)}, u32[]{:S(2)}) collective-permute-start(bf16[128,768]{1,0:T(8,128)(2,1)S(1)} %constant_dynamic-update-slice_fusion.12), channel_id=1, source_target_pairs={{0,4},{2,6},{4,0},{6,2},{8,12},{10,14},{12,8},{14,10},{16,20},{18,... | collective-permute-start | bytes 589832 | tf_op jit(solution)/shard_map/ppermute | solution.py:631
  164.4 14.5 %collective-permute-start.28 = (bf16[128,512]{1,0:T(8,128)(2,1)S(1)}, bf16[128,512]{1,0:T(8,128)(2,1)S(1)}, u32[]{:S(2)}, u32[]{:S(2)}) collective-permute-start(bf16[128,512]{1,0:T(8,128)(2,1)S(1)} %constant_dynamic-slice_fusion.1), channel_id=1, source_target_pairs={{0,8},{2,10},{4,12},{6,14},{8,0},{10,2},{12,4},{14,6},{16,24},{18,... | collective-permute-start | bytes 393224 | tf_op jit(solution)/shard_map/ppermute | solution.py:631
  177.5 13.6 %collective-permute-start.13 = (bf16[256,768]{1,0:T(8,128)(2,1)S(1)}, bf16[256,768]{1,0:T(8,128)(2,1)S(1)}, u32[]{:S(2)}, u32[]{:S(2)}) collective-permute-start(bf16[256,768]{1,0:T(8,128)(2,1)S(1)} %constant_dynamic-update-slice_fusion.11), channel_id=1, source_target_pairs={{0,2},{2,0},{4,6},{6,4},{8,10},{10,8},{12,14},{14,12},{16,18},{18,... | collective-permute-start | bytes 1179656 | tf_op jit(solution)/shard_map/ppermute | solution.py:631
  178.9 6.2 %collective-permute-start.29 = (bf16[64,512]{1,0:T(8,128)(2,1)S(1)}, bf16[64,512]{1,0:T(8,128)(2,1)S(1)}, u32[]{:S(2)}, u32[]{:S(2)}) collective-permute-start(bf16[64,512]{1,0:T(8,128)(2,1)S(1)} %constant_dynamic-slice_fusion), channel_id=1, source_target_pairs={{0,16},{2,18},{4,20},{6,22},{8,24},{10,26},{12,28},{14,30},{16,0},... | collective-permute-start | bytes 196616 | tf_op jit(solution)/shard_map/ppermute | solution.py:631
  185.2 5.9 %collective-permute-start.30 = (bf16[64,512]{1,0:T(8,128)(2,1)S(1)}, bf16[64,512]{1,0:T(8,128)(2,1)S(1)}, u32[]{:S(2)}, u32[]{:S(2)}) collective-permute-start(bf16[64,512]{1,0:T(8,128)(2,1)S(1)} %add_convert_fusion.12), channel_id=1, source_target_pairs={{0,16},{2,18},{4,20},{6,22},{8,24},{10,26},{12,28},{14,30},{16,0},... | collective-permute-start | bytes 196616 | tf_op jit(solution)/shard_map/ppermute | solution.py:631
  187.6 10.0 %collective-permute-start.17 = (bf16[64,2688]{1,0:T(8,128)(2,1)S(1)}, bf16[64,2688]{1,0:T(8,128)(2,1)S(1)}, u32[]{:S(2)}, u32[]{:S(2)}) collective-permute-start(bf16[64,2688]{1,0:T(8,128)(2,1)S(1)} %constant_dynamic-slice_fusion.7), channel_id=1, source_target_pairs={{0,8},{2,10},{4,12},{6,14},{8,0},{10,2},{12,4},{14,6},{16,24},{18,... | collective-permute-start | bytes 1032200 | tf_op jit(solution)/shard_map/ppermute | solution.py:631
  191.1 5.2 %collective-permute-start.31 = (bf16[128,512]{1,0:T(8,128)(2,1)S(1)}, bf16[128,512]{1,0:T(8,128)(2,1)S(1)}, u32[]{:S(2)}, u32[]{:S(2)}) collective-permute-start(bf16[128,512]{1,0:T(8,128)(2,1)S(1)} %constant_dynamic-update-slice_fusion.4), channel_id=1, source_target_pairs={{0,8},{2,10},{4,12},{6,14},{8,0},{10,2},{12,4},{14,6},{16,24},{18,... | collective-permute-start | bytes 393224 | tf_op jit(solution)/shard_map/ppermute | solution.py:631
  191.2 26.0 %collective-permute-start.14 = (bf16[512,768]{1,0:T(8,128)(2,1)S(1)}, bf16[512,768]{1,0:T(8,128)(2,1)S(1)}, u32[]{:S(2)}, u32[]{:S(2)}) collective-permute-start(bf16[512,768]{1,0:T(8,128)(2,1)S(1)} %constant_dynamic-update-slice_fusion.10), channel_id=1, source_target_pairs={{0,1},{1,0},{2,3},{3,2},{4,5},{5,4},{6,7},{7,6},{8,9},{9,8},{10,11... | collective-permute-start | bytes 2359304 | tf_op jit(solution)/shard_map/ppermute | solution.py:617
  196.3 6.4 %collective-permute-start.32 = (bf16[256,512]{1,0:T(8,128)(2,1)S(1)}, bf16[256,512]{1,0:T(8,128)(2,1)S(1)}, u32[]{:S(2)}, u32[]{:S(2)}) collective-permute-start(bf16[256,512]{1,0:T(8,128)(2,1)S(1)} %constant_dynamic-update-slice_fusion.3), channel_id=1, source_target_pairs={{0,4},{2,6},{4,0},{6,2},{8,12},{10,14},{12,8},{14,10},{16,20},{18,... | collective-permute-start | bytes 786440 | tf_op jit(solution)/shard_map/ppermute | solution.py:631
  197.7 7.4 %collective-permute-start.18 = (bf16[32,2688]{1,0:T(8,128)(2,1)S(1)}, bf16[32,2688]{1,0:T(8,128)(2,1)S(1)}, u32[]{:S(2)}, u32[]{:S(2)}) collective-permute-start(bf16[32,2688]{1,0:T(8,128)(2,1)S(1)} %constant_dynamic-slice_fusion.6), channel_id=1, source_target_pairs={{0,2},{2,0},{4,6},{6,4},{8,10},{10,8},{12,14},{14,12},{16,18},{18,... | collective-permute-start | bytes 516104 | tf_op jit(solution)/shard_map/ppermute | solution.py:631
  202.8 39.2 %collective-permute-start.33 = (bf16[512,512]{1,0:T(8,128)(2,1)S(1)}, bf16[512,512]{1,0:T(8,128)(2,1)S(1)}, u32[]{:S(2)}, u32[]{:S(2)}) collective-permute-start(bf16[512,512]{1,0:T(8,128)(2,1)S(1)} %constant_dynamic-update-slice_fusion.2), channel_id=1, source_target_pairs={{0,2},{2,0},{4,6},{6,4},{8,10},{10,8},{12,14},{14,12},{16,18},{18,... | collective-permute-start | bytes 1572872 | tf_op jit(solution)/shard_map/ppermute | solution.py:631
  205.2 6.4 %collective-permute-start.19 = (bf16[16,2688]{1,0:T(8,128)(2,1)S(1)}, bf16[16,2688]{1,0:T(8,128)(2,1)S(1)}, u32[]{:S(2)}, u32[]{:S(2)}) collective-permute-start(bf16[16,2688]{1,0:T(8,128)(2,1)S(1)} %constant_dynamic-slice_fusion.5), channel_id=1, source_target_pairs={{0,16},{2,18},{4,20},{6,22},{8,24},{10,26},{12,28},{14,30},{16,0},... | collective-permute-start | bytes 258056 | tf_op jit(solution)/shard_map/ppermute | solution.py:631
  211.6 5.6 %collective-permute-start.20 = (bf16[16,2688]{1,0:T(8,128)(2,1)S(1)}, bf16[16,2688]{1,0:T(8,128)(2,1)S(1)}, u32[]{:S(2)}, u32[]{:S(2)}) collective-permute-start(bf16[16,2688]{1,0:T(8,128)(2,1)S(1)} %add_convert_fusion.11), channel_id=1, source_target_pairs={{0,16},{2,18},{4,20},{6,22},{8,24},{10,26},{12,28},{14,30},{16,0},... | collective-permute-start | bytes 258056 | tf_op jit(solution)/shard_map/ppermute | solution.py:631
  217.1 5.5 %collective-permute-start.21 = (bf16[32,2688]{1,0:T(8,128)(2,1)S(1)}, bf16[32,2688]{1,0:T(8,128)(2,1)S(1)}, u32[]{:S(2)}, u32[]{:S(2)}) collective-permute-start(bf16[32,2688]{1,0:T(8,128)(2,1)S(1)} %constant_dynamic-update-slice_fusion.9), channel_id=1, source_target_pairs={{0,2},{2,0},{4,6},{6,4},{8,10},{10,8},{12,14},{14,12},{16,18},{18,... | collective-permute-start | bytes 516104 | tf_op jit(solution)/shard_map/ppermute | solution.py:631
  222.6 7.3 %collective-permute-start.22 = (bf16[64,2688]{1,0:T(8,128)(2,1)S(1)}, bf16[64,2688]{1,0:T(8,128)(2,1)S(1)}, u32[]{:S(2)}, u32[]{:S(2)}) collective-permute-start(bf16[64,2688]{1,0:T(8,128)(2,1)S(1)} %constant_dynamic-update-slice_fusion.8), channel_id=1, source_target_pairs={{0,8},{2,10},{4,12},{6,14},{8,0},{10,2},{12,4},{14,6},{16,24},{18,... | collective-permute-start | bytes 1032200 | tf_op jit(solution)/shard_map/ppermute | solution.py:631
  230.0 11.0 %collective-permute-start.23 = (bf16[128,2688]{1,0:T(8,128)(2,1)S(1)}, bf16[128,2688]{1,0:T(8,128)(2,1)S(1)}, u32[]{:S(2)}, u32[]{:S(2)}) collective-permute-start(bf16[128,2688]{1,0:T(8,128)(2,1)S(1)} %constant_dynamic-update-slice_fusion.7), channel_id=1, source_target_pairs={{0,4},{2,6},{4,0},{6,2},{8,12},{10,14},{12,8},{14,10},{16,20},{18,... | collective-permute-start | bytes 2064392 | tf_op jit(solution)/shard_map/ppermute | solution.py:631
  241.1 7.7 %collective-permute-start.24 = (bf16[256,2688]{1,0:T(8,128)(2,1)S(1)}, bf16[256,2688]{1,0:T(8,128)(2,1)S(1)}, u32[]{:S(2)}, u32[]{:S(2)}) collective-permute-start(bf16[256,2688]{1,0:T(8,128)(2,1)S(1)} %constant_dynamic-update-slice_fusion.6), channel_id=1, source_target_pairs={{0,1},{1,0},{2,3},{3,2},{4,5},{5,4},{6,7},{7,6},{8,9},{9,8},{10,11... | collective-permute-start | bytes 4128776 | tf_op jit(solution)/shard_map/ppermute | solution.py:617
  242.0 4.1 %collective-permute-start.34 = (bf16[1024,512]{1,0:T(8,128)(2,1)S(1)}, bf16[1024,512]{1,0:T(8,128)(2,1)S(1)}, u32[]{:S(2)}, u32[]{:S(2)}) collective-permute-start(bf16[1024,512]{1,0:T(8,128)(2,1)S(1)} %constant_dynamic-update-slice_fusion.1), channel_id=1, source_target_pairs={{0,1},{1,0},{2,3},{3,2},{4,5},{5,4},{6,7},{7,6},{8,9},{9,8},{10,11... | collective-permute-start | bytes 3145736 | tf_op jit(solution)/shard_map/ppermute | solution.py:617
  (18 other events, 127.4 us)

commit v2 on v1

--- a/solution.py
+++ b/solution.py
@@ -14,6 +14,7 @@
 MASKED = -1e30
 EPS = 1e-05
 MIB = 1 << 20
+VMEM_MIB = 52
 
 
 def nn(a, b):
@@ -66,16 +67,34 @@
 
 
 def forward_kernel(
-    info, own, other, skip_own, skip_other, query_weight, key_weight, value_weight, gain, shift,
-    mixed_own, mixed_other, query, keys, saved, mixed, logsum, normed, values,
+    info, own_in, other_in, skip_own_in, skip_other_in, query_in, key_in, value_in, gain_in, shift_in,
+    mixed_own_out, mixed_other_out, query_out, keys_out, saved_out, mixed_out, logsum_out, normed_out,
+    own, other, skip_own, skip_other, query_weight, key_weight, value_weight,
+    mixed_own, mixed_other, query, keys, saved, mixed, logsum, normed, values, gain, shift, semaphores,
 ):
     count, head = info[0], info[1]
     half = own.shape[0]
     total = 2 * half
     blocks = total // BLOCK
+    cols = pl.ds(pl.multiple_of(head * 256, 256), 256)
+    fresh_cols = pl.ds(pl.multiple_of(head * 128, 128), 128)
+    mover = Mover(semaphores)
+    mover.start(own_in, own, "own")
+    mover.start(gain_in, gain, "gain")
+    mover.start(shift_in, shift, "shift")
+    mover.start(query_in.at[:, cols], query_weight, "q")
+    mover.start(key_in.at[:, cols], key_weight, "k")
+    mover.start(value_in.at[:, fresh_cols], value_weight, "v")
+    mover.start(skip_own_in.at[:, fresh_cols], skip_own, "skip")
+    mover.start(other_in, other, "other")
+    mover.start(skip_other_in.at[:, fresh_cols], skip_other, "skip_other")
     values[:, :, 128:] = jnp.ones((2, total, 128), BF16)
 
-    for rows_ref, skip_ref, which in ((own, skip_own, head), (other, skip_other, 1 - head)):
+    for rows_ref, skip_ref, which, needs in (
+        (own, skip_own, head, ("own", "gain", "shift", "q", "k", "v", "skip")),
+        (other, skip_other, 1 - head, ("other", "skip_other")),
+    ):
+        mover.wait(*needs)
 
         def project(step, _, rows_ref=rows_ref, skip_ref=skip_ref, which=which):
             at = pl.ds(pl.multiple_of(step * BLOCK, BLOCK), BLOCK)
@@ -119,6 +138,9 @@
             return 0
 
         lax.fori_loop(0, half // BLOCK, project, 0)
+
+    for source, target in ((query, query_out), (keys, keys_out), (saved, saved_out), (normed, normed_out)):
+        mover.start(source, target)
 
     per_slot = blocks // count
     lane = lax.broadcasted_iota(jnp.int32, (1, 128), 1)
@@ -174,8 +196,13 @@
         return 0
 
     lax.fori_loop(0, blocks, attend, 0)
-
-    for out_ref, which in ((mixed_own, head), (mixed_other, 1 - head)):
+    mover.start(mixed, mixed_out)
+    mover.start(logsum, logsum_out)
+
+    for out_ref, target, which in (
+        (mixed_other, mixed_other_out, 1 - head),
+        (mixed_own, mixed_own_out, head),
+    ):
 
         def give(step, _, out_ref=out_ref, which=which):
             at = pl.ds(pl.multiple_of(step * BLOCK, BLOCK), BLOCK)
@@ -193,10 +220,44 @@
             return 0
 
         lax.fori_loop(0, half // BLOCK, give, 0)
-
-
-def whole(shape):
-    return pl.BlockSpec(shape, lambda i, s: (0,) * len(shape))
+        mover.start(out_ref, target)
+    mover.wait_all()
+
+
+class Mover:
+    def __init__(self, semaphores):
+        self.semaphores, self.used, self.open = semaphores, 0, {}
+
+    def start(self, source, target, name=None):
+        copy = pltpu.make_async_copy(source, target, self.semaphores.at[self.used])
+        copy.start()
+        self.open[self.used if name is None else name] = copy
+        self.used += 1
+
+    def wait(self, *names):
+        for name in names:
+            self.open.pop(name).wait()
+
+    def wait_all(self):
+        self.wait(*list(self.open))
+
+
+def run_kernel(kernel, name, scalars, args, outs, scratch, moves, flops, aliases=None):
+    smem = pl.BlockSpec(memory_space=pltpu.SMEM)
+    large = pl.BlockSpec(memory_space=pl.ANY)
+    size = lambda shape, dtype: math.prod(shape) * jnp.dtype(dtype).itemsize
+    moved = sum(size(a.shape, a.dtype) for a in args) + sum(size(*o) for o in outs)
+    return pl.pallas_call(
+        kernel,
+        in_specs=[smem] * len(scalars) + [large] * len(args),
+        out_specs=[large] * len(outs),
+        out_shape=[jax.ShapeDtypeStruct(*o) for o in outs],
+        scratch_shapes=[pltpu.VMEM(*s) for s in scratch] + [pltpu.SemaphoreType.DMA((moves,))],
+        input_output_aliases=aliases or {},
+        cost_estimate=pl.CostEstimate(flops=flops, bytes_accessed=moved, transcendentals=0),
+        compiler_params=pltpu.CompilerParams(vmem_limit_bytes=VMEM_MIB * MIB),
+        name=name,
+    )(*scalars, *args)
 
 
 def forward_attention(info, own, other, skip_own, skip_other, wq, wk, wv, gain, shift):
@@ -213,29 +274,23 @@
         ((2, 8, total), F32),
         ((total, width), BF16),
     ]
-    return pl.pallas_call(
-        forward_kernel,
-        grid_spec=pltpu.PrefetchScalarGridSpec(
-            num_scalar_prefetch=1,
-            grid=(1,),
-            in_specs=[
-                whole(own.shape),
-                whole(other.shape),
-                pl.BlockSpec((half, 128), lambda i, s: (0, s[1])),
-                whole(skip_other.shape),
-                pl.BlockSpec((width, group), lambda i, s: (0, s[1])),
-                pl.BlockSpec((width, group), lambda i, s: (0, s[1])),
-                pl.BlockSpec((width, 128), lambda i, s: (0, s[1])),
-                whole(gain.shape),
-                whole(shift.shape),
-            ],
-            out_specs=[whole(s) for s, _ in outs],
-            scratch_shapes=[pltpu.VMEM((2, total, 256), BF16)],
-        ),
-        out_shape=[jax.ShapeDtypeStruct(s, d) for s, d in outs],
-        compiler_params=pltpu.CompilerParams(vmem_limit_bytes=56 * MIB),
-        name="forward_attention",
-    )(info, own, other, skip_own, skip_other, wq, wk, wv, gain, shift)
+    scratch = [
+        ((half, width), BF16),
+        ((half, width), BF16),
+        ((half, 128), BF16),
+        ((half, 128), BF16),
+        ((width, group), BF16),
+        ((width, group), BF16),
+        ((width, 128), BF16),
+        *outs,
+        ((2, total, 256), BF16),
+        (gain.shape, F32),
+        (shift.shape, F32),
+    ]
+    return run_kernel(
+        forward_kernel, "forward_attention", (info,),
+        (own, other, skip_own, skip_other, wq, wk, wv, gain, shift), outs, scratch, 17, 10 * 10**9,
+    )
 
 
 COLS = 512
@@ -254,11 +309,27 @@
 
 
 def rows_kernel(
-    info, lengths, tokens, mixed_own, mixed_other, cotangent, mixing_weight, expand_weight,
-    shrink_weight, expand_bias, gain, shift,
-    output, after_grad, send_own, send_other, shrink_grad, wide_grad,
-    bias_grad, gain_grads, active, slope, pre_grad, middle, out_grad, after_low,
+    info, lengths, tokens_in, mixed_own_in, mixed_other_in, cotangent_in, mixing_in, expand_in,
+    shrink_in, bias_in, gain_in, shift_in,
+    output_out, after_grad_out, send_own_out, send_other_out, grads_own_out, grads_other_out,
+    tokens, mixed_own, mixed_other, cotangent, mixing_weight, expand_weight, shrink_weight,
+    expand_bias, gain, shift, output, after_grad, send_own, send_other, grads_own, grads_other,
+    bias_grad, gain_grads, active, slope, pre_grad, middle, out_grad, after_low, semaphores,
 ):
+    mover = Mover(semaphores)
+    for source, target, name in (
+        (mixing_in, mixing_weight, "mixing"),
+        (tokens_in, tokens, "tokens"),
+        (mixed_own_in, mixed_own, "own"),
+        (mixed_other_in, mixed_other, "other"),
+        (gain_in, gain, "gain"),
+        (shift_in, shift, "shift"),
+        (bias_in, expand_bias, "bias"),
+        (expand_in, expand_weight, "expand"),
+        (shrink_in, shrink_weight, "shrink"),
+        (cotangent_in, cotangent, "cotangent"),
+    ):
+        mover.start(source, target, name)
     count, head = info[0], info[1]
     half, width = tokens.shape
     hidden = expand_weight.shape[1]
@@ -272,6 +343,7 @@
     there = pl.ds(pl.multiple_of((1 - head) * group, group), group)
     bias_grad[...] = jnp.zeros_like(bias_grad)
     gain_grads[...] = jnp.zeros_like(gain_grads)
+    mover.wait_all()
 
     def tile(step, _):
         at = pl.ds(pl.multiple_of(step * BLOCK, BLOCK), BLOCK)
@@ -322,19 +394,36 @@
 
     lax.fori_loop(0, half // BLOCK, tile, 0)
 
-    def weights(step, _):
-        cs = pl.ds(pl.multiple_of(step * COLS, COLS), COLS)
-        shrink_grad[cs, :] = tn(active[:, cs], out_grad[...]).astype(BF16)
-        wide_grad[:, cs] = tn(middle[...], pre_grad[:, cs]).astype(BF16)
-        return 0
-
-    lax.fori_loop(0, hidden // COLS, weights, 0)
-    mix = slice(hidden, hidden + width)
-    wide_grad[here, mix] = tn(mixed_own[...], after_low[...]).astype(BF16)
-    wide_grad[there, mix] = tn(mixed_other[...], after_low[...]).astype(BF16)
+    for source, target in (
+        (send_other, send_other_out),
+        (send_own, send_own_out),
+        (output, output_out),
+        (after_grad, after_grad_out),
+    ):
+        mover.start(source, target)
     vectors = [bias_grad[0:1, c : c + width] for c in range(0, hidden, width)]
     vectors += [gain_grads[0:1, :], gain_grads[1:2, :]]
-    wide_grad[:, hidden + width :] = as_columns(vectors)
+    vectors += [jnp.zeros_like(vectors[0])] * (16 - len(vectors))
+    vectors = jnp.concatenate(vectors, axis=0).astype(BF16)
+    for grads, target, mixed, which in (
+        (grads_other, grads_other_out, mixed_other, 1 - head),
+        (grads_own, grads_own_out, mixed_own, head),
+    ):
+
+        def weights(step, _, grads=grads, which=which):
+            cs = pl.ds(pl.multiple_of((2 * which + step) * COLS, COLS), COLS)
+            at = pl.multiple_of(step * COLS, COLS)
+            grads[pl.ds(at, COLS), :] = tn(active[:, cs], out_grad[...]).astype(BF16)
+            grads[pl.ds(2 * COLS + at, COLS), :] = tn(middle[...], pre_grad[:, cs]).astype(BF16)
+            return 0
+
+        lax.fori_loop(0, 2, weights, 0)
+        last = 4 * COLS + group
+        grads[4 * COLS : last, :] = tn(mixed[...], after_low[...]).astype(BF16)
+        grads[last : last + 16, :] = vectors
+        grads[last + 16 :, :] = jnp.zeros((112, width), BF16)
+        mover.start(grads, target)
+    mover.wait_all()
 
 
 def row_part(info, lengths, tokens, mixed_own, mixed_other, cotangent, wo, we, ws, bias, gain, shift):
@@ -346,46 +435,30 @@
         ((half, width), F32),
         ((half, group), BF16),
         ((half, group), BF16),
-        ((hidden, width), BF16),
-        ((width, hidden + width + 128), BF16),
+        ((hidden + group + 128, width), BF16),
+        ((hidden + group + 128, width), BF16),
     ]
     args = (tokens, mixed_own, mixed_other, cotangent, wo, we, ws, bias, gain, shift)
-    block = lambda shape: pl.BlockSpec(shape, lambda i, s, t: (0,) * len(shape))
-    return pl.pallas_call(
-        rows_kernel,
-        grid_spec=pltpu.PrefetchScalarGridSpec(
-            num_scalar_prefetch=2,
-            grid=(1,),
-            in_specs=[block(a.shape) for a in args],
-            out_specs=[block(s) for s, _ in outs],
-            scratch_shapes=[
-                pltpu.VMEM((8, hidden), F32),
-                pltpu.VMEM((8, width), F32),
-                pltpu.VMEM((half, hidden), BF16),
-                pltpu.VMEM((BLOCK, hidden), F32),
-                pltpu.VMEM((half, hidden), BF16),
-                pltpu.VMEM((half, width), BF16),
-                pltpu.VMEM((half, width), BF16),
-                pltpu.VMEM((half, width), BF16),
-            ],
-        ),
-        out_shape=[jax.ShapeDtypeStruct(s, d) for s, d in outs],
-        compiler_params=pltpu.CompilerParams(vmem_limit_bytes=60 * MIB),
-        name="row_part",
-    )(info, lengths, *args)
-
-
-def backward_kernel(
-    info, own, other, grad_own, grad_other, query, keys, values, mixed, logsum, normed,
-    query_weight, key_weight, value_weight,
-    weight_grad, back_own, back_other, skip_own, skip_other,
-    gain_grads, grad, inner, query_total, packed, skipped, back,
-):
-    count, head = info[0], info[1]
-    half = own.shape[0]
+    scratch = [
+        *[(a.shape, a.dtype) for a in args],
+        *outs,
+        ((8, hidden), F32),
+        ((8, width), F32),
+        ((half, hidden), BF16),
+        ((BLOCK, hidden), F32),
+        ((half, hidden), BF16),
+        ((half, width), BF16),
+        ((half, width), BF16),
+        ((half, width), BF16),
+    ]
+    return run_kernel(
+        rows_kernel, "row_part", (info, lengths), args, outs, scratch, 16, 15 * 10**9
+    )
+
+
+def arrange_gradient(count, head, grad_own, grad_other, mixed, grad, inner):
+    half = grad_own.shape[0]
     total = 2 * half
-    blocks = total // BLOCK
-    query_total[...] = jnp.zeros_like(query_total)
 
     for rows_ref, which in ((grad_own, head), (grad_other, 1 - head)):
 
@@ -423,8 +496,11 @@
                 )
         return 0
 
-    lax.fori_loop(0, blocks, inners, 0)
-
+    lax.fori_loop(0, total // BLOCK, inners, 0)
+
+
+def attend_blocks(count, first, last, query, keys, values, grad, logsum, inner, query_total, kept):
+    blocks = first + query.shape[1] // BLOCK
     per_slot = blocks // count
     lane = lax.broadcasted_iota(jnp.int32, (1, 128), 1)
     tri = lax.broadcasted_iota(jnp.int32, (BLOCK, BLOCK), 0) <= lax.broadcasted_iota(
@@ -433,11 +509,11 @@
 
     def attend(block, _):
         width = per_slot - block % per_slot
-        here = pl.multiple_of(block * BLOCK, BLOCK)
 
         def run(wide):
+            here = pl.multiple_of((block - first) * BLOCK, BLOCK)
             span = pl.ds(here, wide * BLOCK)
-            at = pl.ds(here, BLOCK)
+            at = out = pl.ds(here, BLOCK)
 
             def score(h):
                 pair, sub = h // 2, h % 2
@@ -466,49 +542,242 @@
                 done.append(finish(h, *now))
                 if h % 2:
                     pair = h // 2
-                    first, second = done[h - 1], done[h]
-                    gv = jnp.where(lane < 64, first[0], second[0]).astype(BF16)
-                    gk = jnp.where(lane < 64, first[1], second[1]).astype(BF16)
-                    packed[at, 256 + pair * 128 : 256 + (pair + 1) * 128] = gk
-                    if pair == 0:
-                        packed[at, 512:] = gv
-                    else:
-                        skipped[at, :] = gv
-                    query_total[pair, span, :] += first[2] + second[2]
-
-        for wide in range(1, blocks + 1):
+                    one, two = done[h - 1], done[h]
+                    kept[out, pair * 128 : (pair + 1) * 128] = jnp.where(
+                        lane < 64, one[1], two[1]
+                    ).astype(BF16)
+                    kept[out, 256 + pair * 128 : 256 + (pair + 1) * 128] = jnp.where(
+                        lane < 64, one[0], two[0]
+                    ).astype(BF16)
+                    query_total[pair, span, :] += one[2] + two[2]
+
+        for wide in range(1, blocks - first + 1):
             pl.when(width == wide)(partial(run, wide))
         return 0
 
-    lax.fori_loop(0, blocks, attend, 0)
+    lax.fori_loop(first, last, attend, 0)
+
+
+def first_kernel(
+    last, info, grad_own_in, grad_other_in, query_in, keys_in, values_in, mixed_in, logsum_in,
+    grad_out, inner_out, query_total_out, kept_out,
+    grad_own, grad_other, query, keys, values, mixed, logsum, grad, inner, query_total, kept, semaphores,
+):
+    mover = Mover(semaphores)
+    rows = pl.ds(0, last * BLOCK)
+    mover.start(grad_own_in, grad_own, "a")
+    mover.start(grad_other_in, grad_other, "b")
+    mover.start(mixed_in, mixed, "c")
+    mover.start(query_in, query, "d")
+    mover.start(keys_in.at[:, rows], keys, "e")
+    mover.start(values_in.at[:, rows], values, "f")
+    mover.start(logsum_in, logsum, "g")
+    query_total[...] = jnp.zeros_like(query_total)
+    mover.wait("a", "b", "c")
+    arrange_gradient(info[0], info[1], grad_own, grad_other, mixed, grad, inner)
+    mover.start(grad, grad_out)
+    mover.start(inner, inner_out)
+    mover.wait("d", "e", "f", "g")
+    attend_blocks(info[0], 0, last, query, keys, values, grad, logsum, inner, query_total, kept)
+    mover.start(query_total, query_total_out)
+    mover.start(kept, kept_out)
+    mover.wait_all()
+
+
+def first_blocks(last, info, grad_own, grad_other, query, keys, values, mixed, logsum):
+    total = query.shape[1]
+    outs = [
+        ((2, total, 128), BF16),
+        ((2, 8, total), F32),
+        ((2, total, 128), F32),
+        ((last * BLOCK, 512), BF16),
+    ]
+    scratch = [
+        (grad_own.shape, BF16),
+        (grad_other.shape, BF16),
+        (query.shape, BF16),
+        ((2, last * BLOCK, 128), BF16),
+        ((2, last * BLOCK, 128), BF16),
+        (mixed.shape, BF16),
+        (logsum.shape, F32),
+        *outs,
+    ]
+    return run_kernel(
+        partial(first_kernel, last), "first_blocks", (info,),
+        (grad_own, grad_other, query, keys, values, mixed, logsum), outs, scratch, 11, 10**10,
+    )
+
+
+def fetch_blocks(mover, first, last, sources, targets):
+    before, query, keys, values, grad, logsum, inner = sources
+    total = query.shape[1]
+    span, rows = pl.ds(first * BLOCK, total - first * BLOCK), pl.ds(first * BLOCK, (last - first) * BLOCK)
+    for source, target in zip(
+        (
+            keys.at[:, rows], query.at[:, span], values.at[:, rows], grad.at[:, span],
+            logsum.at[:, :, span], inner.at[:, :, span], before.at[:, span],
+        ),
+        targets,
+    ):
+        mover.start(source, target)
+
+
+def next_kernel(first, last, info, *refs):
+    sources, (query_total_out, kept_out), local, (kept, semaphores) = (
+        refs[:7], refs[7:9], refs[9:16], refs[16:]
+    )
+    mover = Mover(semaphores)
+    fetch_blocks(mover, first, last, sources, local)
+    mover.wait_all()
+    keys, query, values, grad, logsum, inner, query_total = local
+    attend_blocks(
+        info[0], first, last, query, keys, values, grad, logsum, inner, query_total, kept
+    )
+    total = sources[1].shape[1]
+    span = pl.ds(first * BLOCK, total - first * BLOCK)
+    mover.start(query_total, query_total_out.at[:, span])
+    mover.start(kept, kept_out)
+    mover.wait_all()
+
+
+def local_blocks(first, last, total):
+    rows, span = (last - first) * BLOCK, total - first * BLOCK
+    return [
+        ((2, rows, 128), BF16),
+        ((2, span, 128), BF16),
+        ((2, rows, 128), BF16),
+        ((2, span, 128), BF16),
+        ((2, 8, span), F32),
+        ((2, 8, span), F32),
+        ((2, span, 128), F32),
+    ]
+
+
+def next_blocks(first, last, info, before, query, keys, values, grad, logsum, inner):
+    outs = [(before.shape, F32), (((last - first) * BLOCK, 512), BF16)]
+    return run_kernel(
+        partial(next_kernel, first, last), f"blocks_{first}", (info,),
+        (before, query, keys, values, grad, logsum, inner), outs,
+        local_blocks(first, last, query.shape[1]) + [outs[1]], 9, 5 * 10**9, {1: 0},
+    )
+
+
+def last_kernel(first, pieces, info, *refs):
+    sources, refs = refs[:7], refs[7:]
+    normed_in, gain_in, shift_in, query_in, key_in, value_in = refs[:6]
+    kept_in, refs = refs[6 : 6 + pieces], refs[6 + pieces :]
+    weight_grad_out, packed_out = refs[:2]
+    local, refs = refs[2:9], refs[9:]
+    kept, normed, gain, shift, query_weight, key_weight, value_weight, before, weight_grad, packed, semaphores = refs
+    keys, query, values, grad, logsum, inner, query_total = local
+    total = packed.shape[0]
+    head = info[1]
+    cols = pl.ds(pl.multiple_of(head * 256, 256), 256)
+    fresh_cols = pl.ds(pl.multiple_of(head * 128, 128), 128)
+    mover = Mover(semaphores)
+    fetch_blocks(mover, first, total // BLOCK, sources, local)
+    mover.start(sources[0].at[:, pl.ds(0, first * BLOCK)], before, "before")
+    mover.start(normed_in, normed, "normed")
+    mover.start(gain_in, gain, "gain")
+    mover.start(shift_in, shift, "shift")
+    mover.start(query_in.at[:, cols], query_weight, "q")
+    mover.start(key_in.at[:, cols], key_weight, "k")
+    mover.start(value_in.at[:, fresh_cols], value_weight, "v")
+    row = 0
+    for n, piece in enumerate(kept_in):
+        mover.start(piece, packed.at[pl.ds(row, piece.shape[0]), pl.ds(256, 512)], f"p{n}")
+        row += piece.shape[0]
+    mover.wait(*range(7))
+    attend_blocks(
+        info[0], first, total // BLOCK, query, keys, values, grad, logsum, inner, query_total, kept
+    )
+    mover.wait_all()
+    packed[row:, 256:] = kept[...]
+    for pair in range(2):
+        lanes = slice(pair * 128, (pair + 1) * 128)
+        packed[:row, lanes] = (before[pair, :, :] * 0.125).astype(BF16)
+        packed[row:, lanes] = (query_total[pair, :, :] * 0.125).astype(BF16)
+    mover.start(packed, packed_out)
+    ones = jnp.ones((8, total), BF16)
+    gain_grad = jnp.zeros((gain.shape[1], 1), F32)
+    shift_grad = jnp.zeros((gain.shape[1], 1), F32)
+    gain_column = jnp.transpose(jnp.broadcast_to(gain[...], (128, gain.shape[1])))[:, :1]
+    shift_column = jnp.transpose(jnp.broadcast_to(shift[...], (128, gain.shape[1])))[:, :1]
+    for start, stop, weight in ((0, 256, query_weight), (256, 512, key_weight), (512, 640, value_weight)):
+        part = packed[:, start:stop]
+        product = tn(normed[...], part)
+        sums = nn(ones, part)[0:1, :]
+        weight_grad[:, start:stop] = product.astype(BF16)
+        weight = weight[...].astype(F32)
+        shift_grad += jnp.sum(weight * sums, axis=1, keepdims=True)
+        gain_grad += jnp.sum(weight * (product - shift_column * sums), axis=1, keepdims=True)
+    lane = lax.broadcasted_iota(jnp.int32, (1, 128), 1)
+    edge = jnp.where(lane == 0, gain_grad / gain_column, jnp.where(lane == 1, shift_grad, 0.0))
+    weight_grad[:, 640:] = edge.astype(BF16)
+    mover.start(weight_grad, weight_grad_out)
+    mover.wait_all()
+
+
+def last_blocks(first, info, before, query, keys, values, grad, logsum, inner, normed, gain, shift, wq, wk, wv, kept):
+    total, width = normed.shape
+    outs = [((width, 768), BF16), ((total, 768), BF16)]
+    scratch = local_blocks(first, total // BLOCK, total) + [
+        ((total - first * BLOCK, 512), BF16),
+        (normed.shape, BF16),
+        (gain.shape, F32),
+        (shift.shape, F32),
+        ((width, 256), BF16),
+        ((width, 256), BF16),
+        ((width, 128), BF16),
+        ((2, first * BLOCK, 128), F32),
+        *outs,
+    ]
+    return run_kernel(
+        partial(last_kernel, first, len(kept)), "last_blocks", (info,),
+        (before, query, keys, values, grad, logsum, inner, normed, gain, shift, wq, wk, wv, *kept),
+        outs, scratch, 16 + len(kept), 5 * 10**9,
+    )
+
+
+def back_kernel(
+    info, packed_in, query_in, key_in, value_in, back_own_out, back_other_out, skip_own_out, skip_other_out,
+    packed, query_weight, key_weight, value_weight, back_own, back_other, skip_own, skip_other, back, semaphores,
+):
+    count, head = info[0], info[1]
+    total = packed.shape[0]
+    half = total // 2
+    cols = pl.ds(pl.multiple_of(head * 256, 256), 256)
+    fresh_cols = pl.ds(pl.multiple_of(head * 128, 128), 128)
+    mover = Mover(semaphores)
+    mover.start(packed_in, packed)
+    mover.start(query_in.at[:, cols], query_weight)
+    mover.start(key_in.at[:, cols], key_weight)
+    mover.start(value_in.at[:, fresh_cols], value_weight)
+    mover.wait_all()
 
     def close(block, _):
         at = pl.ds(pl.multiple_of(block * BLOCK, BLOCK), BLOCK)
-        for pair in range(2):
-            packed[at, pair * 128 : (pair + 1) * 128] = (query_total[pair, at, :] * 0.125).astype(BF16)
         back[at, :] = (
             nt(packed[at, :256], query_weight[...])
             + nt(packed[at, 256:512], key_weight[...])
-            + nt(packed[at, 512:], value_weight[...])
+            + nt(packed[at, 512:640], value_weight[...])
         ).astype(BF16)
         return 0
 
-    lax.fori_loop(0, blocks, close, 0)
-    weight_grad[:, :640] = tn(normed[...], packed[...]).astype(BF16)
-    gain_grads[...] = jnp.zeros_like(gain_grads)
-
-    for rows_ref, back_ref, skip_ref, which in (
-        (own, back_own, skip_own, head),
-        (other, back_other, skip_other, 1 - head),
+    lax.fori_loop(0, total // BLOCK, close, 0)
+
+    for back_ref, skip_ref, back_out, skip_out, which in (
+        (back_other, skip_other, back_other_out, skip_other_out, 1 - head),
+        (back_own, skip_own, back_own_out, skip_own_out, head),
     ):
 
-        def give(step, _, rows_ref=rows_ref, back_ref=back_ref, skip_ref=skip_ref, which=which):
+        def give(step, _, back_ref=back_ref, skip_ref=skip_ref, which=which):
             at = pl.ds(pl.multiple_of(step * BLOCK, BLOCK), BLOCK)
             tile = which * (half // BLOCK) + step
 
             def put(count_here):
                 g = load_grouped(lambda s: back[s, :], tile, total, count_here)
-                k = load_grouped(lambda s: skipped[s, :], tile, total, count_here)
+                k = load_grouped(lambda s: packed[s, 640:], tile, total, count_here)
                 if count_here > 1:
                     order = sorter(count_here, True)
                     g = nn(order, g).astype(BF16)
@@ -518,60 +787,47 @@
 
             for option in SLOT_OPTIONS:
                 pl.when(count == option)(partial(put, option))
-            hat, _s = normalized(rows_ref[at, :].astype(F32))
-            g = back_ref[at, :].astype(F32)
-            gain_grads[0:1, :] += jnp.sum(g * hat, axis=0, keepdims=True)
-            gain_grads[1:2, :] += jnp.sum(g, axis=0, keepdims=True)
             return 0
 
         lax.fori_loop(0, half // BLOCK, give, 0)
-    weight_grad[:, 640:] = as_columns([gain_grads[0:1, :], gain_grads[1:2, :]])
-
-
-def backward_attention(
-    info, own, other, grad_own, grad_other, query, keys, values, mixed, logsum, normed, wq, wk, wv
+        mover.start(back_ref, back_out)
+        mover.start(skip_ref, skip_out)
+    mover.wait_all()
+
+
+def back_rows(info, packed, wq, wk, wv):
+    total, width = packed.shape[0], wq.shape[0]
+    half = total // 2
+    outs = [((half, width), BF16), ((half, width), BF16), ((half, 128), BF16), ((half, 128), BF16)]
+    scratch = [
+        (packed.shape, BF16),
+        ((width, 256), BF16),
+        ((width, 256), BF16),
+        ((width, 128), BF16),
+        *outs,
+        ((total, width), BF16),
+    ]
+    return run_kernel(
+        back_kernel, "back_rows", (info,), (packed, wq, wk, wv), outs, scratch, 8, 2 * 10**9
+    )
+
+
+def close_kernel(
+    info, tokens_in, after_grad_in, back_own_in, back_other_in, kept_in, arrived_in, gain_in,
+    result_out, skip_out,
+    tokens, after_grad, back_own, back_other, gain, result, skip_grad, semaphores,
 ):
-    half, width = own.shape
-    total = 2 * half
-    group = wq.shape[1] // 2
-    outs = [
-        ((width, 768), BF16),
-        ((half, width), BF16),
-        ((half, width), BF16),
-        ((half, 128), BF16),
-        ((half, 128), BF16),
-    ]
-    args = (own, other, grad_own, grad_other, query, keys, values, mixed, logsum, normed)
-    return pl.pallas_call(
-        backward_kernel,
-        grid_spec=pltpu.PrefetchScalarGridSpec(
-            num_scalar_prefetch=1,
-            grid=(1,),
-            in_specs=[whole(a.shape) for a in args]
-            + [
-                pl.BlockSpec((width, group), lambda i, s: (0, s[1])),
-                pl.BlockSpec((width, group), lambda i, s: (0, s[1])),
-                pl.BlockSpec((width, 128), lambda i, s: (0, s[1])),
-            ],
-            out_specs=[whole(s) for s, _ in outs],
-            scratch_shapes=[
-                pltpu.VMEM((8, width), F32),
-                pltpu.VMEM((2, total, 128), BF16),
-                pltpu.VMEM((2, 8, total), F32),
-                pltpu.VMEM((2, total, 128), F32),
-                pltpu.VMEM((total, 640), BF16),
-                pltpu.VMEM((total, 128), BF16),
-                pltpu.VMEM((total, width), BF16),
-            ],
-        ),
-        out_shape=[jax.ShapeDtypeStruct(s, d) for s, d in outs],
-        compiler_params=pltpu.CompilerParams(vmem_limit_bytes=60 * MIB),
-        name="backward_attention",
-    )(info, *args, wq, wk, wv)
-
-
-def close_kernel(info, tokens, after_grad, back_own, back_other, gain, kept, arrived, result, skip_grad):
     head = info[1]
+    mover = Mover(semaphores)
+    mover.start(gain_in, gain)
+    mover.start(tokens_in, tokens)
+    mover.start(after_grad_in, after_grad)
+    mover.start(back_own_in, back_own)
+    mover.start(back_other_in, back_other)
+    mover.start(kept_in, skip_grad.at[:, pl.ds(pl.multiple_of(head * 128, 128), 128)])
+    mover.start(arrived_in, skip_grad.at[:, pl.ds(pl.multiple_of((1 - head) * 128, 128), 128)])
+    mover.wait_all()
+    mover.start(skip_grad, skip_out)
 
     def tile(step, _):
         at = pl.ds(pl.multiple_of(step * BLOCK, BLOCK), BLOCK)
@@ -589,28 +845,88 @@
         return 0
 
     lax.fori_loop(0, tokens.shape[0] // BLOCK, tile, 0)
-    skip_grad[:, pl.ds(pl.multiple_of(head * 128, 128), 128)] = kept[...]
-    skip_grad[:, pl.ds(pl.multiple_of((1 - head) * 128, 128), 128)] = arrived[...]
-
-
-def close_rows(info, tokens, after_grad, back_own, back_other, gain, kept, arrived):
-    args = (tokens, after_grad, back_own, back_other, gain, kept, arrived)
-    half = tokens.shape[0]
-    return pl.pallas_call(
-        close_kernel,
-        grid_spec=pltpu.PrefetchScalarGridSpec(
-            num_scalar_prefetch=1,
-            grid=(1,),
-            in_specs=[whole(a.shape) for a in args],
-            out_specs=[whole(tokens.shape), whole((half, 256))],
-        ),
-        out_shape=[
-            jax.ShapeDtypeStruct(tokens.shape, BF16),
-            jax.ShapeDtypeStruct((half, 256), BF16),
-        ],
-        compiler_params=pltpu.CompilerParams(vmem_limit_bytes=32 * MIB),
-        name="close_rows",
-    )(info, *args)
+    mover.start(result, result_out)
+    mover.wait_all()
+
+
+def close_rows(info, tokens, after_grad, back_own, back_other, kept, arrived, gain):
+    args = (tokens, after_grad, back_own, back_other, kept, arrived, gain)
+    outs = [(tokens.shape, BF16), ((tokens.shape[0], 256), BF16)]
+    scratch = [(a.shape, a.dtype) for a in args[:4]] + [(gain.shape, F32)] + outs
+    return run_kernel(close_kernel, "close_rows", (info,), args, outs, scratch, 9, 10**8)
+
+
+def unpack_kernel(
+    info, mine_in, arrived_in, shrink_out, expand_out, mixing_out, bias_out, gain_out, shift_out,
+    mine, arrived, wide, bias, gain, shift, semaphores,
+):
+    head = info[1]
+    width = mine.shape[1]
+    mover = Mover(semaphores)
+    mover.start(mine_in, mine, "mine")
+    mover.start(arrived_in, arrived, "arrived")
+    for half, name, slot, which in ((mine, "mine", 0, head), (arrived, "arrived", 1, 1 - head)):
+        mover.wait(name)
+        for at in range(0, 2 * COLS, COLS):
+            wide[slot, at : at + COLS, :] = half[at : at + COLS, :].astype(F32)
+            row = pl.multiple_of(which * 2 * COLS + at, COLS)
+            mover.start(wide.at[slot, pl.ds(at, COLS)], shrink_out.at[pl.ds(row, COLS)])
+        for at in range(2 * COLS, 4 * COLS, COLS):
+            wide[slot, at : at + COLS, :] = half[at : at + COLS, :].astype(F32)
+            col = pl.multiple_of(which * 2 * COLS + at - 2 * COLS, COLS)
+            mover.start(wide.at[slot, pl.ds(at, COLS)], expand_out.at[:, pl.ds(col, COLS)])
+        top = 4 * COLS + mixing_out.shape[0] // 2
+        wide[slot, 4 * COLS : top + 16, :] = half[4 * COLS : top + 16, :].astype(F32)
+        row = pl.multiple_of(which * (top - 4 * COLS), 256)
+        mover.start(wide.at[slot, pl.ds(4 * COLS, top - 4 * COLS)], mixing_out.at[pl.ds(row, top - 4 * COLS)])
+    vectors = wide[head, top : top + 8, :]
+    for n in range(4):
+        bias[:, n * width : (n + 1) * width] = vectors[n : n + 1]
+    gain[...] = vectors[4:5]
+    shift[...] = vectors[5:6]
+    for source, target in ((bias, bias_out), (gain, gain_out), (shift, shift_out)):
+        mover.start(source, target)
+    mover.wait_all()
+
+
+def unpack_grads(info, mine, arrived):
+    rows, width = mine.shape
+    hidden = 4 * COLS
+    outs = [((hidden, width), F32), ((width, hidden), F32), ((width, width), F32)]
+    small = [((1, hidden), F32), ((1, width), F32), ((1, width), F32)]
+    outs += small
+    scratch = [(mine.shape, BF16), (mine.shape, BF16), ((2, rows, width), F32)] + small
+    return run_kernel(unpack_kernel, "unpack_grads", (info,), (mine, arrived), outs, scratch, 15, 10**8)
+
+
+def split_kernel(
+    info, mine_in, arrived_in, query_out, key_out, value_out, gain_out, shift_out,
+    mine, arrived, query, key, value, gain, shift, semaphores,
+):
+    head = info[1]
+    mover = Mover(semaphores)
+    mover.start(mine_in, mine)
+    mover.start(arrived_in, arrived)
+    mover.wait_all()
+    for half, which in ((mine, head), (arrived, 1 - head)):
+        for target, wide, at in ((query, 256, 0), (key, 256, 256), (value, 128, 512)):
+            cols = pl.ds(pl.multiple_of(which * wide, 128), wide)
+            target[:, cols] = half[:, at : at + wide].astype(F32)
+    for source, target in ((query, query_out), (key, key_out), (value, value_out)):
+        mover.start(source, target)
+    edges = jnp.transpose(mine[:, 640:].astype(F32) + arrived[:, 640:].astype(F32))
+    gain[...] = edges[0:1]
+    shift[...] = edges[1:2]
+    mover.start(gain, gain_out)
+    mover.start(shift, shift_out)
+    mover.wait_all()
+
+
+def split_projection(info, mine, arrived):
+    width = mine.shape[0]
+    outs = [((width, 512), F32), ((width, 512), F32), ((width, 256), F32), ((1, width), F32), ((1, width), F32)]
+    scratch = [(mine.shape, BF16), (mine.shape, BF16)] + outs
+    return run_kernel(split_kernel, "split_projection", (info,), (mine, arrived), outs, scratch, 7, 10**8)
 
 
 def swap_cores(array):
@@ -626,41 +942,66 @@
     return (a.astype(F32) + b.astype(F32)).astype(BF16)
 
 
-def swap_bit(array, bit):
-    size = lax.axis_size("seq")
-    return lax.ppermute(array, "seq", [(i, i ^ (1 << bit)) for i in range(size)])
-
-
-def bit_of(bit):
-    return (lax.axis_index("seq") >> bit) & 1
-
-
 def join(mine, theirs, which):
     both = jnp.concatenate([mine, mine], axis=0)
     return lax.dynamic_update_slice_in_dim(both, theirs, (1 - which) * mine.shape[0], 0)
 
 
-def seq_sum(chunks, first_bits):
-    bits = lax.axis_size("seq").bit_length() - 1
-    orders = [[(f + s) % min(3, bits) for s in range(min(3, bits))] + list(range(3, bits)) for f in first_bits]
-    trail = [[] for _ in chunks]
-    for stage in range(bits):
-        after = []
-        for chunk, order, path in zip(chunks, orders, trail):
-            bit = order[stage]
-            if chunk.shape[0] % 32 == 0:
-                mine = bit_of(bit)
-                path.append(bit)
-                after.append(add_low(half_of(chunk, mine), swap_bit(half_of(chunk, 1 - mine), bit)))
-            else:
-                after.append(add_low(chunk, swap_bit(chunk, bit)))
-        chunks = after
-    while any(trail):
-        for n, path in enumerate(trail):
-            if path:
-                bit = path.pop()
-                chunks[n] = join(chunks[n], swap_bit(chunks[n], bit), bit_of(bit))
-    return chunks
+def after_all(first, *rest):
+    return lax.optimization_barrier((first, *rest))
+
+
+class SeqSum:
+    def __init__(self, mine, coming, orders):
+        self.size = lax.axis_size("seq")
+        bits = self.size.bit_length() - 1
+        self.orders = [
+            [b for b in order if b < bits] + [b for b in range(bits) if b not in order]
+            for order in orders
+        ]
+        self.mine, self.coming, self.stage, self.bits, self.trail = mine, coming, 0, bits, []
+
+    def which(self, stage):
+        bit = jnp.where(lax.axis_index("head") == 0, self.orders[0][stage], self.orders[1][stage])
+        return (lax.axis_index("seq") >> bit) & 1
+
+    def swap(self, array, stage):
+        pairs = []
+        for i in range(self.size):
+            for core in range(2):
+                pairs.append((2 * i + core, 2 * (i ^ (1 << self.orders[core][stage])) + core))
+        return lax.ppermute(array, ("seq", "head"), pairs)
+
+    def added(self, which=None):
+        parts = [a if which is None else half_of(a, which) for a in (self.mine, self.coming) if a is not None]
+        return parts[0] if len(parts) == 1 else add_low(*parts)
+
+    def ready(self):
+        if self.stage < self.bits - 1 and self.mine.shape[0] % 32 == 0:
+            which = self.which(self.stage)
+            self.trail.append(self.stage)
+            self.away, self.mine = self.added(1 - which), self.added(which)
+        else:
+            self.away = self.mine = self.added()
+
+    def send(self):
+        self.coming = self.swap(self.away, self.stage)
+        self.stage += 1
+
+    def finish(self):
+        self.mine, self.coming = self.added(), None
+
+    def call_back(self):
+        self.back_stage = self.trail.pop()
+        self.coming = self.swap(self.mine, self.back_stage)
+
+    def fit(self):
+        self.mine = join(self.mine, self.coming, self.which(self.back_stage))
+
+
+ORDERS = ((0, 1, 2, 3), (1, 2, 3, 0))
+PROJECTION_ORDERS = ((1, 0, 2, 3), (2, 1, 0, 3))
+CUTS = (1, 3, 5, 8)
 
 
 def on_device(
@@ -674,49 +1015,106 @@
     row = lambda v: v.reshape(1, -1)
 
     other = swap_cores(tokens)
-    skip_other = swap_cores(lax.dynamic_slice_in_dim(first_values, (1 - head) * 128, 128, 1))
+    skip_other = swap_cores(first_values)
     mixed_own, mixed_away, query, keys, values, mixed, logsum, normed = forward_attention(
         info, tokens, other, first_values, skip_other, query_weight, key_weight, value_weight,
         row(before_gain), row(before_shift),
     )
     mixed_other = swap_cores(mixed_away)
-    output, after_grad, grad_own, grad_away, shrink_part, wide_part = row_part(
+    output, after_grad, grad_own, grad_away, grads_own, grads_away = row_part(
         info, lengths, tokens, mixed_own, mixed_other, cotangent, mixing_weight, expand_weight,
         shrink_weight, row(expand_bias), row(middle_gain), row(middle_shift),
     )
     grad_other = swap_cores(grad_away)
-    shrink_half = add_low(half_of(shrink_part, head), swap_cores(half_of(shrink_part, 1 - head)))
-    wide_half = add_low(half_of(wide_part, head), swap_cores(half_of(wide_part, 1 - head)))
-    shrink_half, wide_half = seq_sum([shrink_half, wide_half], (0, 1))
-
-    projection_part, back_own, back_away, skip_own, skip_away = backward_attention(
-        info, tokens, other, grad_own, grad_other, query, keys, values, mixed, logsum, normed,
-        query_weight, key_weight, value_weight,
-    )
-    back_other = swap_cores(back_away)
-    skip_arrived = swap_cores(skip_away)
-    (projection,) = seq_sum([projection_part], (0,))
+    grad_other, grads_away = after_all(grad_other, grads_away)
+    grads_come = swap_cores(grads_away)
+    grad, inner, query_total, kept = first_blocks(
+        CUTS[0], info, grad_own, grad_other, query, keys, values, mixed, logsum
+    )
+    pieces = [kept]
+    query_total, grads_come = after_all(query_total, grads_come)
+    sums = SeqSum(grads_own, grads_come, ORDERS)
+    for first, last in zip(CUTS, CUTS[1:-1]):
+        sums.ready()
+        query_total, sums.away = after_all(query_total, sums.away)
+        sums.send()
+        query_total, kept = next_blocks(
+            first, last, info, query_total, query, keys, values, grad, logsum, inner
+        )
+        pieces.append(kept)
+        query_total, sums.coming = after_all(query_total, sums.coming)
+    sums.ready()
+    query_total, sums.away = after_all(query_total, sums.away)
+    sums.send()
+    projection_part, packed = last_blocks(
+        CUTS[-2], info, query_total, query, keys, values, grad, logsum, inner, normed,
+        row(before_gain), row(before_shift), query_weight, key_weight, value_weight, pieces,
+    )
+    projection = SeqSum(projection_part, None, PROJECTION_ORDERS)
+    packed, sums.coming = after_all(packed, sums.coming)
+
+    def both_ready():
+        projection.ready()
+        if sums.stage < sums.bits:
+            sums.ready()
+            return True
+        return False
+
+    more = both_ready()
+    packed, projection.away, sums.away = after_all(packed, projection.away, sums.away)
+    projection.send()
+    if more:
+        sums.send()
+    back_own, back_away, skip_own, skip_away = back_rows(
+        info, packed, query_weight, key_weight, value_weight
+    )
+    while sums.stage < sums.bits or projection.stage < projection.bits - 3:
+        back_away, projection.coming, sums.coming = after_all(
+            back_away, projection.coming, sums.coming
+        )
+        more = both_ready()
+        projection.send()
+        if more:
+            sums.send()
+    back_away, projection.coming, sums.coming = after_all(back_away, projection.coming, sums.coming)
+    back_other, skip_arrived = swap_cores(back_away), swap_cores(skip_away)
+    sums.finish()
+    projection.ready()
+    projection.send()
+    sums.call_back()
+    back_other, projection.coming, sums.coming = after_all(back_other, projection.coming, sums.coming)
+    sums.fit()
+    projection.ready()
+    projection.send()
+    sums.call_back()
     input_grad, skip_grad = close_rows(
-        info, tokens, after_grad, back_own, back_other, row(before_gain), skip_own, skip_arrived
-    )
-    shrink_grad = join(shrink_half, swap_cores(shrink_half), head).astype(F32)
-    wide = join(wide_half, swap_cores(wide_half), head)
-    hidden, width = shrink_grad.shape
-    expand_grad = wide[:, :hidden].astype(F32)
-    mixing_grad = wide[:, hidden : hidden + width].astype(F32)
-    tail = wide[:, hidden + width : hidden + width + 8].astype(F32)
-    bias_grad = tail[:, : hidden // width].T.reshape(hidden)
-    middle_gain_grad, middle_shift_grad = tail[:, 4], tail[:, 5]
-    arrived = swap_cores(projection)
-    low_head = jnp.where(head == 0, projection, arrived).astype(F32)
-    high_head = jnp.where(head == 0, arrived, projection).astype(F32)
-    query_grad = jnp.concatenate([low_head[:, :256], high_head[:, :256]], axis=1)
-    key_grad = jnp.concatenate([low_head[:, 256:512], high_head[:, 256:512]], axis=1)
-    value_grad = jnp.concatenate([low_head[:, 512:640], high_head[:, 512:640]], axis=1)
-    edges = low_head[:, 640:642] + high_head[:, 640:642]
+        info, tokens, after_grad, back_own, back_other, skip_own, skip_arrived, row(before_gain)
+    )
+    input_grad, projection.coming, sums.coming = after_all(input_grad, projection.coming, sums.coming)
+    sums.fit()
+    projection.ready()
+    projection.send()
+    sums.call_back()
+    projection.finish()
+    while len(projection.trail) > 1:
+        projection.call_back()
+        projection.fit()
+    projection.call_back()
+    projection.coming, sums.coming = after_all(projection.coming, sums.coming)
+    while True:
+        sums.fit()
+        if not sums.trail:
+            break
+        sums.call_back()
+    projection.fit()
+    sums_arrived, arrived = swap_cores(sums.mine), swap_cores(projection.mine)
+    shrink_grad, expand_grad, mixing_grad, *sums_vectors = unpack_grads(info, sums.mine, sums_arrived)
+    query_grad, key_grad, value_grad, *edges = split_projection(info, projection.mine, arrived)
+    bias_grad, middle_gain_grad, middle_shift_grad = [v.reshape(-1) for v in sums_vectors]
+    before_gain_grad, before_shift_grad = [v.reshape(-1) for v in edges]
     return (
         output, input_grad, skip_grad, query_grad, key_grad, value_grad, mixing_grad, expand_grad,
-        shrink_grad, bias_grad, edges[:, 0], edges[:, 1], middle_gain_grad, middle_shift_grad,
+        shrink_grad, bias_grad, before_gain_grad, before_shift_grad, middle_gain_grad, middle_shift_grad,
     )
 
 

time: 258 us -> 217 us (0.84)
  waiting for transfers between devices: 95.7 us -> 52.9 us
  Pallas kernels: 108 us -> 127 us
  starting transfers between devices: 24.6 us -> 11.5 us
  other arithmetic: 13.5 us -> 8.92 us
    ppermute x24 -> x14, waiting for transfers between devices: 91.8 us -> 41.8 us  [swap(): return lax.ppermute(array, ('seq', 'head'), pairs)]
    pallas_call x4 -> x10, Pallas kernels: 108 us -> 127 us  [run_kernel(): pl.pallas_call(kernel, in_specs=[smem] * len(scalars) + [large] * len(arg...]
    ppermute x24 -> x14, starting transfers between devices: 21.5 us -> 8.99 us  [swap(): return lax.ppermute(array, ('seq', 'head'), pairs)]
    ppermute x11 -> x9, waiting for transfers between devices: 3.85 us -> 11.1 us  [swap_cores(): return lax.ppermute(array, 'head', [(0, 1), (1, 0)])]
    convert_element_type x5 -> x0, other arithmetic: 6.57 us -> none  [the longest x1 2.6 us: on_device(): shrink_grad = join(shrink_half, swap_cores(shrink_half), head).astype(F32)]
    convert_element_type x14 -> x9, other arithmetic: 2.49 us -> 8.41 us  [add_low(): return (a.astype(F32) + b.astype(F32)).astype(BF16)]
    unnamed x31 -> x52, local copies, waits for them, and re-layouts: 3.31 us -> 8.39 us
    concatenate x3 -> x0, other arithmetic: 3.08 us -> none  [the longest x1 1.12 us: on_device(): jnp.concatenate([low_head[:, 256:512], high_head[:, 256:512]], axis=1)]
  transfers between devices with their start and end apart: 35 -> 23, of which waited for: 20 -> 14; matrix products, arithmetic and copies ran while one was open for 6% -> 2% of each run, Pallas kernels for 1% -> 33%
where the time goes in v2:
time: 217 us; the launch traced here: 213 us
  Pallas kernels  127 us (59%)
  waiting for transfers between devices  52.9 us (24%)
  starting transfers between devices  11.5 us (5%)
  local copies, waits for them, and re-layouts  10.7 us (5%)
  other arithmetic  8.92 us (4%)
    pallas_call x10, Pallas kernels, run_kernel(): pl.pallas_call(kernel, in_specs=[smem] * len(scalars) + [large] * len(arg...  127 us
    ppermute x14, waiting for transfers between devices, swap(): return lax.ppermute(array, ('seq', 'head'), pairs)  41.8 us
    ppermute x9, waiting for transfers between devices, swap_cores(): return lax.ppermute(array, 'head', [(0, 1), (1, 0)])  11.1 us
    ppermute x14, starting transfers between devices, swap(): return lax.ppermute(array, ('seq', 'head'), pairs)  8.99 us
    convert_element_type x9, other arithmetic, add_low(): return (a.astype(F32) + b.astype(F32)).astype(BF16)  8.41 us
    unnamed x52, local copies, waits for them, and re-layouts  8.39 us
  transfers between devices with their start and end apart: 23, of which 14 were waited for; matrix products, arithmetic and copies ran while one was open for 2% of the time, Pallas kernels for 33%

profile of v2, /device:TPU:0, one launch (start us, length us, event | category | flops | bytes accessed | tf_op | source)
XLA Modules:
  0.0 212.9 jit_solution(2245225923500512479)
XLA Ops:
  2.0 2.4 %collective-permute-done.1.skip_other_in = bf16[1024,256]{1,0:T(8,128)(2,1)S(1)} collective-permute-done((bf16[1024,256]{1,0:T(8,128)(2,1)}, bf16[1024,256]{1,0:T(8,128)(2,1)S(1)}, u32[]{:S(2)}, u32[]{:S(2)}) %collective-permute-start.1) | collective-permute-done | bytes 524320 | tf_op jit(solution)/shard_map/ppermute | solution.py:933
  6.2 1.0 copy-done.3
  8.9 23.2 %forward_attention.1 = (bf16[1024,256]{1,0:T(8,128)(2,1)S(1)}, bf16[1024,256]{1,0:T(8,128)(2,1)S(1)}, bf16[2,2048,128]{2,1,0:T(8,128)(2,1)}, bf16[2,2048,128]{2,...) custom-call(s32[2]{0:T(128)S(1)} %pad_add_fusion.info, ...), custom_call_target="tpu_custom_call" | custom-call | flops 10000000000 | bytes 11931648 | tf_op jit(solution)/shard_map/forward_attention/pallas_call | solution.py:250
  32.5 1.5 collective-permute-done.2.mixed_other_in
  34.9 26.7 %row_part.1 = (bf16[1024,512]{1,0:T(8,128)(2,1)}, f32[1024,512]{1,0:T(8,128)}, bf16[1024,256]{1,0:T(8,128)(2,1)S(1)}, bf16[1024,256]{1,0:T(8,128)(2,1)S(1)}, bf1...) custom-call(s32[2]{0:T(128)S(1)} %pad_add_fusion.info, s32[8]{0:T(128)S(1)} %bitcast.20, bf16[1024,512]{1,0:T(8,128)(2,1)} %tokens_in.3, ...), custom_call_target="tpu_custom_call" | custom-call | flops 15000000512 | bytes 17051648 | tf_op jit(solution)/shard_map/row_part/pallas_call | solution.py:250
  62.0 1.5 collective-permute-done.3.grad_other_in
  63.9 20.1 %first_blocks.1 = (bf16[2,2048,128]{2,1,0:T(8,128)(2,1)}, f32[2,8,2048]{2,1,0:T(8,128)S(1)}, f32[2,2048,128]{2,1,0:T(8,128)}, bf16[256,512]{1,0:T(8,128)(2,1)S(1)}) custom-call(s32[2]{0:T(128)S(1)} %pad_add_fusion.info, bf16[1024,256]{1,0:T(8,128)(2,1)S(1)} %get-tuple-element.89.grad_own_in, bf16[1024,256]{1,0:T(8,128)(2,1)S(1)} %collective-permute-done.3.grad_other_in, ...), custom_call_target="tpu_custom_call" | custom-call | flops 10000000000 | bytes 8912896 | tf_op jit(solution)/shard_map/first_blocks/pallas_call | solution.py:250
  84.0 3.5 %add_convert_fusion = (bf16[1216,512]{1,0:T(8,128)(2,1)S(1)}, bf16[1216,512]{1,0:T(8,128)(2,1)}) fusion(bf16[2432,512]{1,0:T(8,128)(2,1)} %collective-permute-done.4, s32[]{:T(128)S(6)} %select_n.81, bf16[2432,512]{1,0:T(8,128)(2,1)S(1)} %copy-done.19, s32[]{:T(128)S(6)} %select_n.80), kind=kLoop, calls=%fused_computation.1 | loop fusion | flops 4980736 | bytes 7471112 | tf_op jit(solution)/shard_map/convert_element_type | solution.py:942
  87.5 14.4 %blocks_1.1 = (f32[2,2048,128]{2,1,0:T(8,128)}, bf16[512,512]{1,0:T(8,128)(2,1)S(1)}) custom-call(s32[2]{0:T(128)S(1)} %pad_add_fusion.info, f32[2,2048,128]{2,1,0:T(8,128)} %get-tuple-element.103.refs_0_, bf16[2,2048,128]{2,1,0:T(8,128)(2,1)S(1)} %copy-done.14, ...), custom_call_target="tpu_custom_call", output_to_operand_aliasing={{0}: (1, {})} | custom-call | flops 5000000000 | bytes 9175040 | tf_op jit(solution)/shard_map/blocks_1/pallas_call | solution.py:250
  102.7 2.0 collective-permute-done.5
  104.8 2.4 %add_convert_fusion.2 = (bf16[608,512]{1,0:T(8,128)(2,1)S(1)}, bf16[608,512]{1,0:T(8,128)(2,1)}) fusion(bf16[1216,512]{1,0:T(8,128)(2,1)} %collective-permute-done.5, s32[]{:T(128)S(6)} %select_n.84, bf16[1216,512]{1,0:T(8,128)(2,1)S(1)} %get-tuple-element.156, s32[]{:T(128)S(6)} %select_n.83), kind=kLoop, calls=%fused_computation.4 | loop fusion | flops 2490368 | bytes 3735560 | tf_op jit(solution)/shard_map/convert_element_type | solution.py:942
  107.2 10.3 %blocks_3.1 = (f32[2,2048,128]{2,1,0:T(8,128)}, bf16[512,512]{1,0:T(8,128)(2,1)S(1)}) custom-call(s32[2]{0:T(128)S(1)} %pad_add_fusion.info, f32[2,2048,128]{2,1,0:T(8,128)} %get-tuple-element.110.refs_0_, bf16[2,2048,128]{2,1,0:T(8,128)(2,1)S(1)} %copy-done.14, ...), custom_call_target="tpu_custom_call", output_to_operand_aliasing={{0}: (1, {})} | custom-call | flops 5000000000 | bytes 9175040 | tf_op jit(solution)/shard_map/blocks_3/pallas_call | solution.py:250
  118.4 4.3 %collective-permute-start.7 = (bf16[304,512]{1,0:T(8,128)(2,1)S(1)}, bf16[304,512]{1,0:T(8,128)(2,1)S(1)}, u32[]{:S(2)}, u32[]{:S(2)}) collective-permute-start(bf16[304,512]{1,0:T(8,128)(2,1)S(1)} %add_convert_fusion.7), channel_id=1, source_target_pairs={{0,8},{1,17},{2,10},{3,19},{4,12},{5,21},{6,14},{7,23},{8,0},{9,25... | collective-permute-start | bytes 933896 | tf_op jit(solution)/shard_map/ppermute | solution.py:973
  122.7 11.5 %last_blocks.1 = (bf16[512,768]{1,0:T(8,128)(2,1)}, bf16[2048,768]{1,0:T(8,128)(2,1)}) custom-call(s32[2]{0:T(128)S(1)} %pad_add_fusion.info, f32[2,2048,128]{2,1,0:T(8,128)} %get-tuple-element.115.refs_0_, bf16[2,2048,128]{2,1,0:T(8,128)(2,1)} %get-tuple-element.93.query_in.refs_1_, bf16[2,2048,128]{2,1,0:T(8,128)(2,1)} %get-tuple-element.94.keys_in.refs_2_, ...), custom_call_target="tpu_custom_call" | custom-call | flops 5000000000 | bytes 15208448 | tf_op jit(solution)/shard_map/last_blocks/pallas_call | solution.py:250
  136.0 7.2 %back_rows.1 = (bf16[1024,512]{1,0:T(8,128)(2,1)}, bf16[1024,512]{1,0:T(8,128)(2,1)}, bf16[1024,128]{1,0:T(8,128)(2,1)S(1)}, bf16[1024,128]{1,0:T(8,128)(2,1)S(1)}) custom-call(s32[2]{0:T(128)S(1)} %pad_add_fusion.info, bf16[2048,768]{1,0:T(8,128)(2,1)} %get-tuple-element.125.packed_in, bf16[512,512]{1,0:T(8,128)(2,1)S(1)} %copy-done.4, ...), custom_call_target="tpu_custom_call" | custom-call | flops 2000000000 | bytes 7077888 | tf_op jit(solution)/shard_map/back_rows/pallas_call | solution.py:250
  143.3 3.4 %collective-permute-done.9 = bf16[304,512]{1,0:T(8,128)(2,1)S(1)} collective-permute-done((bf16[304,512]{1,0:T(8,128)(2,1)S(1)}, bf16[304,512]{1,0:T(8,128)(2,1)S(1)}, u32[]{:S(2)}, u32[]{:S(2)}) %collective-permute-start.9) | collective-permute-done | bytes 311328 | tf_op jit(solution)/shard_map/ppermute | solution.py:973
  146.8 1.2 add_convert_fusion.8
  148.2 5.6 %collective-permute-done.11 = bf16[128,768]{1,0:T(8,128)(2,1)S(1)} collective-permute-done((bf16[128,768]{1,0:T(8,128)(2,1)S(1)}, bf16[128,768]{1,0:T(8,128)(2,1)S(1)}, u32[]{:S(2)}, u32[]{:S(2)}) %collective-permute-start.11) | collective-permute-done | bytes 196640 | tf_op jit(solution)/shard_map/ppermute | solution.py:973
  153.8 3.3 %collective-permute-done.12 = bf16[304,512]{1,0:T(8,128)(2,1)S(1)} collective-permute-done((bf16[304,512]{1,0:T(8,128)(2,1)S(1)}, bf16[304,512]{1,0:T(8,128)(2,1)S(1)}, u32[]{:S(2)}, u32[]{:S(2)}) %collective-permute-start.12) | collective-permute-done | bytes 311328 | tf_op jit(solution)/shard_map/ppermute | solution.py:973
  157.1 1.8 collective-permute-start.15
  160.4 5.3 %close_rows.1 = (bf16[1024,512]{1,0:T(8,128)(2,1)}, bf16[1024,256]{1,0:T(8,128)(2,1)}) custom-call(s32[2]{0:T(128)S(1)} %pad_add_fusion.info, bf16[1024,512]{1,0:T(8,128)(2,1)S(1)} %copy-done, f32[1024,512]{1,0:T(8,128)} %get-tuple-element.88.after_grad_in, bf16[1024,512]{1,0:T(8,128)(2,1)} %get-tuple-element.126.back_own_in, bf16[1024,512]{1,0:T(8,128)(2,1)} %copy-done.20, ...), custom_call_target="tpu_custom_call" | custom-call | flops 100000000 | bytes 7342080 | tf_op jit(solution)/shard_map/close_rows/pallas_call | solution.py:250
  165.7 1.8 collective-permute-done.15
  167.7 1.1 constant_dynamic-update-slice_fusion.2
  168.9 5.7 %collective-permute-done.16 = bf16[64,768]{1,0:T(8,128)(2,1)S(1)} collective-permute-done((bf16[64,768]{1,0:T(8,128)(2,1)S(1)}, bf16[64,768]{1,0:T(8,128)(2,1)S(1)}, u32[]{:S(2)}, u32[]{:S(2)}) %collective-permute-start.16) | collective-permute-done | bytes 98336 | tf_op jit(solution)/shard_map/ppermute | solution.py:973
  174.7 4.6 %collective-permute-done.17 = bf16[64,768]{1,0:T(8,128)(2,1)S(1)} collective-permute-done((bf16[64,768]{1,0:T(8,128)(2,1)S(1)}, bf16[64,768]{1,0:T(8,128)(2,1)S(1)}, u32[]{:S(2)}, u32[]{:S(2)}) %collective-permute-start.17) | collective-permute-done | bytes 98336 | tf_op jit(solution)/shard_map/ppermute | solution.py:973
  179.4 9.5 %collective-permute-done.18 = bf16[128,768]{1,0:T(8,128)(2,1)S(1)} collective-permute-done((bf16[128,768]{1,0:T(8,128)(2,1)S(1)}, bf16[128,768]{1,0:T(8,128)(2,1)S(1)}, u32[]{:S(2)}, u32[]{:S(2)}) %collective-permute-start.18) | collective-permute-done | bytes 196640 | tf_op jit(solution)/shard_map/ppermute | solution.py:973
  189.0 1.7 collective-permute-start.19
  190.9 5.9 %collective-permute-done.19 = bf16[256,768]{1,0:T(8,128)(2,1)S(1)} collective-permute-done((bf16[256,768]{1,0:T(8,128)(2,1)S(1)}, bf16[256,768]{1,0:T(8,128)(2,1)S(1)}, u32[]{:S(2)}, u32[]{:S(2)}) %collective-permute-start.19) | collective-permute-done | bytes 393248 | tf_op jit(solution)/shard_map/ppermute | solution.py:973
  197.7 5.2 %collective-permute-done.21.arrived_in = bf16[512,768]{1,0:T(8,128)(2,1)S(1)} collective-permute-done((bf16[512,768]{1,0:T(8,128)(2,1)S(1)}, bf16[512,768]{1,0:T(8,128)(2,1)S(1)}, u32[]{:S(2)}, u32[]{:S(2)}) %collective-permute-start.21) | collective-permute-done | bytes 786464 | tf_op jit(solution)/shard_map/ppermute | solution.py:933
  202.9 2.3 %split_projection.1 = (f32[512,512]{1,0:T(8,128)}, f32[512,512]{1,0:T(8,128)}, f32[512,256]{1,0:T(8,128)}, f32[1,512]{1,0:T(1,128)}, f32[1,512]{1,0:T(1,128)}) custom-call(s32[2]{0:T(128)S(1)} %pad_add_fusion.info, bf16[512,768]{1,0:T(8,128)(2,1)S(1)} %constant_dynamic-update-slice_fusion.5.mine_in, bf16[512,768]{1,0:T(8,128)(2,1)S(1)} %collective-permute-done.21.arrived_in), custom_call_target="tpu_custom_call" | custom-call | flops 100000000 | bytes 4198400 | tf_op jit(solution)/shard_map/split_projection/pallas_call | solution.py:250
  205.2 1.5 copy-done.18
  206.7 6.0 %unpack_grads.1 = (f32[2048,512]{1,0:T(8,128)}, f32[512,2048]{1,0:T(8,128)}, f32[512,512]{1,0:T(8,128)}, f32[1,2048]{1,0:T(1,128)}, f32[1,512]{1,0:T(1,128)}, /*index=5*/f32[1,512]{1,0:T(1,128)}) custom-call(s32[2]{0:T(128)S(1)} %pad_add_fusion.info, bf16[2432,512]{1,0:T(8,128)(2,1)} %copy-done.17, bf16[2432,512]{1,0:T(8,128)(2,1)} %copy-done.18), custom_call_target="tpu_custom_call" | custom-call | flops 100000000 | bytes 14430208 | tf_op jit(solution)/shard_map/unpack_grads/pallas_call | solution.py:250
  (99 shorter events, 13.1 us)
Async XLA Ops:
  0.6 3.8 %collective-permute-start = (bf16[1024,512]{1,0:T(8,128)(2,1)}, bf16[1024,512]{1,0:T(8,128)(2,1)S(1)}, u32[]{:S(2)}, u32[]{:S(2)}) collective-permute-start(bf16[1024,512]{1,0:T(8,128)(2,1)} %tokens_in.3), channel_id=1, source_target_pairs={{0,1},{1,0},{2,3},{3,2},{4,5},{5,4},{6,7},{7,6},{8,9},{9,8},{10,11... | collective-permute-start | bytes 3145736 | tf_op jit(solution)/shard_map/ppermute | solution.py:933
  1.2 3.2 %collective-permute-start.1 = (bf16[1024,256]{1,0:T(8,128)(2,1)}, bf16[1024,256]{1,0:T(8,128)(2,1)S(1)}, u32[]{:S(2)}, u32[]{:S(2)}) collective-permute-start(bf16[1024,256]{1,0:T(8,128)(2,1)} %skip_own_in.1), channel_id=1, source_target_pairs={{0,1},{1,0},{2,3},{3,2},{4,5},{5,4},{6,7},{7,6},{8,9},{9,8},{10,11... | collective-permute-start | bytes 1572872 | tf_op jit(solution)/shard_map/ppermute | solution.py:933
  8.9 26.0 %copy-start.8 = (f32[2048]{0:T(1024)S(1)}, f32[2048]{0:T(1024)}, u32[]{:S(2)}) copy-start(f32[2048]{0:T(1024)} %param.27) | copy-start | bytes 24580
  8.9 26.0 %copy-start.9 = (f32[512]{0:T(512)S(1)}, f32[512]{0:T(512)}, u32[]{:S(2)}) copy-start(f32[512]{0:T(512)} %param.30) | copy-start | bytes 6148
  8.9 26.0 %copy-start.10 = (f32[512]{0:T(512)S(1)}, f32[512]{0:T(512)}, u32[]{:S(2)}) copy-start(f32[512]{0:T(512)} %param.31) | copy-start | bytes 6148
  8.9 26.0 %copy-start.13 = (s32[1,8]{1,0:T(1,128)S(1)}, s32[1,8]{1,0:T(1,128)}, u32[]{:S(2)}) copy-start(s32[1,8]{1,0:T(1,128)} %param.20) | copy-start | bytes 100
  32.1 2.0 collective-permute-start.2
  61.6 2.0 collective-permute-start.3
  63.6 20.4 %collective-permute-start.4 = (bf16[2432,512]{1,0:T(8,128)(2,1)}, bf16[2432,512]{1,0:T(8,128)(2,1)}, u32[]{:S(2)}, u32[]{:S(2)}) collective-permute-start(bf16[2432,512]{1,0:T(8,128)(2,1)} %get-tuple-element.99), channel_id=1, source_target_pairs={{0,1},{1,0},{2,3},{3,2},{4,5},{5,4},{6,7},{7,6},{8,9},{9,8},{10,11... | collective-permute-start | bytes 7471112 | tf_op jit(solution)/shard_map/ppermute | solution.py:933
  63.9 20.1 %copy-start.19 = (bf16[2432,512]{1,0:T(8,128)(2,1)S(1)}, bf16[2432,512]{1,0:T(8,128)(2,1)}, u32[]{:S(2)}) copy-start(bf16[2432,512]{1,0:T(8,128)(2,1)} %get-tuple-element.101) | copy-start | bytes 7471108
  87.5 17.2 %collective-permute-start.5 = (bf16[1216,512]{1,0:T(8,128)(2,1)}, bf16[1216,512]{1,0:T(8,128)(2,1)}, u32[]{:S(2)}, u32[]{:S(2)}) collective-permute-start(bf16[1216,512]{1,0:T(8,128)(2,1)} %get-tuple-element.107), channel_id=1, source_target_pairs={{0,2},{1,5},{2,0},{3,7},{4,6},{5,1},{6,4},{7,3},{8,10},{9,13},{10,... | collective-permute-start | bytes 3735560 | tf_op jit(solution)/shard_map/ppermute | solution.py:973
  107.2 11.1 %collective-permute-start.6 = (bf16[608,512]{1,0:T(8,128)(2,1)}, bf16[608,512]{1,0:T(8,128)(2,1)S(1)}, u32[]{:S(2)}, u32[]{:S(2)}) collective-permute-start(bf16[608,512]{1,0:T(8,128)(2,1)} %get-tuple-element.112), channel_id=1, source_target_pairs={{0,4},{1,9},{2,6},{3,11},{4,0},{5,13},{6,2},{7,15},{8,12},{9,1},{1... | collective-permute-start | bytes 1867784 | tf_op jit(solution)/shard_map/ppermute | solution.py:973
  107.2 15.5 %copy-start.2 = (f32[512]{0:T(512)S(1)}, f32[512]{0:T(512)}, u32[]{:S(2)}) copy-start(f32[512]{0:T(512)} %param.28) | copy-start | bytes 6148
  107.2 15.5 %copy-start.4 = (bf16[512,512]{1,0:T(8,128)(2,1)S(1)}, bf16[512,512]{1,0:T(8,128)(2,1)}, u32[]{:S(2)}) copy-start(bf16[512,512]{1,0:T(8,128)(2,1)} %query_in.3) | copy-start | bytes 1572868
  107.2 15.5 %copy-start.5 = (bf16[512,512]{1,0:T(8,128)(2,1)S(1)}, bf16[512,512]{1,0:T(8,128)(2,1)}, u32[]{:S(2)}) copy-start(bf16[512,512]{1,0:T(8,128)(2,1)} %key_in.3) | copy-start | bytes 1572868
  107.2 15.5 %copy-start.7 = (bf16[512,256]{1,0:T(8,128)(2,1)S(1)}, bf16[512,256]{1,0:T(8,128)(2,1)}, u32[]{:S(2)}) copy-start(bf16[512,256]{1,0:T(8,128)(2,1)} %value_in.3) | copy-start | bytes 786436
  118.4 16.9 %collective-permute-start.7 = (bf16[304,512]{1,0:T(8,128)(2,1)S(1)}, bf16[304,512]{1,0:T(8,128)(2,1)S(1)}, u32[]{:S(2)}, u32[]{:S(2)}) collective-permute-start(bf16[304,512]{1,0:T(8,128)(2,1)S(1)} %add_convert_fusion.7), channel_id=1, source_target_pairs={{0,8},{1,17},{2,10},{3,19},{4,12},{5,21},{6,14},{7,23},{8,0},{9,25... | collective-permute-start | bytes 933896 | tf_op jit(solution)/shard_map/ppermute | solution.py:973
  135.4 11.3 %collective-permute-start.8 = (bf16[256,768]{1,0:T(8,128)(2,1)S(1)}, bf16[256,768]{1,0:T(8,128)(2,1)S(1)}, u32[]{:S(2)}, u32[]{:S(2)}) collective-permute-start(bf16[256,768]{1,0:T(8,128)(2,1)S(1)} %constant_dynamic-slice_fusion), channel_id=1, source_target_pairs={{0,4},{1,9},{2,6},{3,11},{4,0},{5,13},{6,2},{7,15},{8,12},{9,1},{1... | collective-permute-start | bytes 1179656 | tf_op jit(solution)/shard_map/ppermute | solution.py:973
  135.5 11.2 %collective-permute-start.9 = (bf16[304,512]{1,0:T(8,128)(2,1)S(1)}, bf16[304,512]{1,0:T(8,128)(2,1)S(1)}, u32[]{:S(2)}, u32[]{:S(2)}) collective-permute-start(bf16[304,512]{1,0:T(8,128)(2,1)S(1)} %add_convert_fusion.5), channel_id=1, source_target_pairs={{0,16},{1,3},{2,18},{3,1},{4,20},{5,7},{6,22},{7,5},{8,24},{9,11},... | collective-permute-start | bytes 933896 | tf_op jit(solution)/shard_map/ppermute | solution.py:973
  146.7 10.4 %collective-permute-start.10 = (bf16[1024,512]{1,0:T(8,128)(2,1)}, bf16[1024,512]{1,0:T(8,128)(2,1)S(1)}, u32[]{:S(2)}, u32[]{:S(2)}) collective-permute-start(bf16[1024,512]{1,0:T(8,128)(2,1)} %get-tuple-element.130), channel_id=1, source_target_pairs={{0,1},{1,0},{2,3},{3,2},{4,5},{5,4},{6,7},{7,6},{8,9},{9,8},{10,11... | collective-permute-start | bytes 3145736 | tf_op jit(solution)/shard_map/ppermute | solution.py:933
  146.7 10.3 %collective-permute-start.12 = (bf16[304,512]{1,0:T(8,128)(2,1)S(1)}, bf16[304,512]{1,0:T(8,128)(2,1)S(1)}, u32[]{:S(2)}, u32[]{:S(2)}) collective-permute-start(bf16[304,512]{1,0:T(8,128)(2,1)S(1)} %add_convert_fusion.4), channel_id=1, source_target_pairs={{0,8},{1,17},{2,10},{3,19},{4,12},{5,21},{6,14},{7,23},{8,0},{9,25... | collective-permute-start | bytes 933896 | tf_op jit(solution)/shard_map/ppermute | solution.py:973
  148.0 5.7 %collective-permute-start.11 = (bf16[128,768]{1,0:T(8,128)(2,1)S(1)}, bf16[128,768]{1,0:T(8,128)(2,1)S(1)}, u32[]{:S(2)}, u32[]{:S(2)}) collective-permute-start(bf16[128,768]{1,0:T(8,128)(2,1)S(1)} %get-tuple-element.161), channel_id=1, source_target_pairs={{0,2},{1,5},{2,0},{3,7},{4,6},{5,1},{6,4},{7,3},{8,10},{9,13},{10,... | collective-permute-start | bytes 589832 | tf_op jit(solution)/shard_map/ppermute | solution.py:973
  157.1 10.4 %collective-permute-start.15 = (bf16[608,512]{1,0:T(8,128)(2,1)S(1)}, bf16[608,512]{1,0:T(8,128)(2,1)}, u32[]{:S(2)}, u32[]{:S(2)}) collective-permute-start(bf16[608,512]{1,0:T(8,128)(2,1)S(1)} %constant_dynamic-update-slice_fusion), channel_id=1, source_target_pairs={{0,4},{1,9},{2,6},{3,11},{4,0},{5,13},{6,2},{7,15},{8,12},{9,1},{1... | collective-permute-start | bytes 1867784 | tf_op jit(solution)/shard_map/ppermute | solution.py:973
  158.9 1.5 collective-permute-start.13
  159.8 5.9 %collective-permute-start.14 = (bf16[64,768]{1,0:T(8,128)(2,1)S(1)}, bf16[64,768]{1,0:T(8,128)(2,1)S(1)}, u32[]{:S(2)}, u32[]{:S(2)}) collective-permute-start(bf16[64,768]{1,0:T(8,128)(2,1)S(1)} %add_convert_fusion.13), channel_id=1, source_target_pairs={{0,8},{1,3},{2,10},{3,1},{4,12},{5,7},{6,14},{7,5},{8,0},{9,11},{1... | collective-permute-start | bytes 294920 | tf_op jit(solution)/shard_map/ppermute | solution.py:973
  167.5 7.0 %collective-permute-start.16 = (bf16[64,768]{1,0:T(8,128)(2,1)S(1)}, bf16[64,768]{1,0:T(8,128)(2,1)S(1)}, u32[]{:S(2)}, u32[]{:S(2)}) collective-permute-start(bf16[64,768]{1,0:T(8,128)(2,1)S(1)} %add_convert_fusion.11), channel_id=1, source_target_pairs={{0,16},{1,17},{2,18},{3,19},{4,20},{5,21},{6,22},{7,23},{8,24},{9,... | collective-permute-start | bytes 294920 | tf_op jit(solution)/shard_map/ppermute | solution.py:973
  168.8 28.0 %collective-permute-start.20 = (bf16[1216,512]{1,0:T(8,128)(2,1)S(1)}, bf16[1216,512]{1,0:T(8,128)(2,1)S(1)}, u32[]{:S(2)}, u32[]{:S(2)}) collective-permute-start(bf16[1216,512]{1,0:T(8,128)(2,1)S(1)} %constant_dynamic-update-slice_fusion.2), channel_id=1, source_target_pairs={{0,2},{1,5},{2,0},{3,7},{4,6},{5,1},{6,4},{7,3},{8,10},{9,13},{10,... | collective-permute-start | bytes 3735560 | tf_op jit(solution)/shard_map/ppermute | solution.py:973
  174.6 4.7 %collective-permute-start.17 = (bf16[64,768]{1,0:T(8,128)(2,1)S(1)}, bf16[64,768]{1,0:T(8,128)(2,1)S(1)}, u32[]{:S(2)}, u32[]{:S(2)}) collective-permute-start(bf16[64,768]{1,0:T(8,128)(2,1)S(1)} %add_convert_fusion.10), channel_id=1, source_target_pairs={{0,8},{1,3},{2,10},{3,1},{4,12},{5,7},{6,14},{7,5},{8,0},{9,11},{1... | collective-permute-start | bytes 294920 | tf_op jit(solution)/shard_map/ppermute | solution.py:973
  179.3 9.7 %collective-permute-start.18 = (bf16[128,768]{1,0:T(8,128)(2,1)S(1)}, bf16[128,768]{1,0:T(8,128)(2,1)S(1)}, u32[]{:S(2)}, u32[]{:S(2)}) collective-permute-start(bf16[128,768]{1,0:T(8,128)(2,1)S(1)} %constant_dynamic-update-slice_fusion.1), channel_id=1, source_target_pairs={{0,2},{1,5},{2,0},{3,7},{4,6},{5,1},{6,4},{7,3},{8,10},{9,13},{10,... | collective-permute-start | bytes 589832 | tf_op jit(solution)/shard_map/ppermute | solution.py:973
  189.0 7.8 %collective-permute-start.19 = (bf16[256,768]{1,0:T(8,128)(2,1)S(1)}, bf16[256,768]{1,0:T(8,128)(2,1)S(1)}, u32[]{:S(2)}, u32[]{:S(2)}) collective-permute-start(bf16[256,768]{1,0:T(8,128)(2,1)S(1)} %constant_dynamic-update-slice_fusion.3), channel_id=1, source_target_pairs={{0,4},{1,9},{2,6},{3,11},{4,0},{5,13},{6,2},{7,15},{8,12},{9,1},{1... | collective-permute-start | bytes 1179656 | tf_op jit(solution)/shard_map/ppermute | solution.py:973
  197.0 8.2 %collective-permute-start.22 = (bf16[2432,512]{1,0:T(8,128)(2,1)S(1)}, bf16[2432,512]{1,0:T(8,128)(2,1)S(1)}, u32[]{:S(2)}, u32[]{:S(2)}) collective-permute-start(bf16[2432,512]{1,0:T(8,128)(2,1)S(1)} %constant_dynamic-update-slice_fusion.4.mine_in), channel_id=1, source_target_pairs={{0,1},{1,0},{2,3},{3,2},{4,5},{5,4},{6,7},{7,6},{8,9},{9,8},{10,11... | collective-permute-start | bytes 7471112 | tf_op jit(solution)/shard_map/ppermute | solution.py:933
  197.2 5.7 %collective-permute-start.21 = (bf16[512,768]{1,0:T(8,128)(2,1)S(1)}, bf16[512,768]{1,0:T(8,128)(2,1)S(1)}, u32[]{:S(2)}, u32[]{:S(2)}) collective-permute-start(bf16[512,768]{1,0:T(8,128)(2,1)S(1)} %constant_dynamic-update-slice_fusion.5.mine_in), channel_id=1, source_target_pairs={{0,1},{1,0},{2,3},{3,2},{4,5},{5,4},{6,7},{7,6},{8,9},{9,8},{10,11... | collective-permute-start | bytes 2359304 | tf_op jit(solution)/shard_map/ppermute | solution.py:933
  (17 other events, 62.5 us)
